TPU v7x, 32 devices: a whole 2x2x4 slice. The times are simulated.
32 devices in a mesh: wide: 8 (over z, x), narrow: 4 (over y, core).
Axes of the slice: x: 2, y: 2, z: 4, core: 2. Of those that a mesh axis runs over, the one named last changes fastest.
Arguments:
- rhs: float32 [64, 64, 1024], P(None, 'wide', 'narrow'), may hold values from -6 to 6
- areas: float32 [64, 1024], P('wide', 'narrow'), may hold values from 0.5 to 2
- stiffness: float32 [64], replicated, may hold values from 1e-07 to 1
Outputs:
- pressure: float32 [64, 64, 1024], P(None, 'wide', 'narrow')
- residual: float32 [64, 64, 1024], P(None, 'wide', 'narrow')
All inputs are finite; a program needn't handle non-finite values.
Results may differ from a plain program's by a relative error of at most 0.0003.
Values sent between devices are 32-bit elements; how exact they have to be, the bound alone decides.
A program may use at most 64 MiB of HBM per device.

v0:
```python
import jax
import jax.numpy as jnp
from jax import lax
from jax.sharding import PartitionSpec as P

coupling = 2.0
relaxation = 0.4


def extended(cells, sides, width):
    for axis, dim in sides:
        count = lax.axis_size(axis)
        ends = count - 1
        head = lax.slice_in_dim(cells, 0, width, axis=dim)
        tail = lax.slice_in_dim(cells, cells.shape[dim] - width, cells.shape[dim], axis=dim)
        cells = jnp.concatenate(
            [
                lax.ppermute(tail, axis, [(i, (i + 1) % count) for i in range(ends)]),
                cells,
                lax.ppermute(head, axis, [((i + 1) % count, i) for i in range(ends)]),
            ],
            axis=dim,
        )
    return cells


def entering_2(array, axis, combine, identity, reverse):
    peers, here = (lax.axis_size(axis), lax.axis_index(axis))
    everything = jax.tree.map(lambda part: lax.all_gather(part, axis), array)
    start = jax.tree.map(
        lambda part, zero: jnp.broadcast_to(jnp.asarray(zero, part.dtype), part.shape),
        array,
        identity,
    )

    def turn(k, before):
        at = peers - 1 - k if reverse else k
        reached = at > here if reverse else at < here
        new = combine(before, jax.tree.map(lambda part: part[at], everything))
        return jax.tree.map(lambda a, b: jnp.where(reached, a, b), new, before)

    return lax.fori_loop(0, peers, turn, start)


def column_inverse(stiffness):
    levels = stiffness.shape[0]
    identity_k = jnp.eye(levels, dtype=stiffness.dtype)
    neighbours = jnp.eye(levels, k=1, dtype=stiffness.dtype) + jnp.eye(
        levels, k=-1, dtype=stiffness.dtype
    )
    matrix = jnp.diag(stiffness + 2.0 * coupling + 4.0) - coupling * neighbours
    lower = jnp.linalg.cholesky(matrix)
    lower_inv = lax.linalg.triangular_solve(lower, identity_k, left_side=True, lower=True)
    return jnp.dot(lower_inv.T, lower_inv, precision=lax.Precision.HIGHEST)


def apply_columns(inverse, field):
    return jnp.einsum("kl,lxy->kxy", inverse, field, precision=lax.Precision.HIGHEST)


def vertical(field, stiffness):
    empty = jnp.zeros_like(field[:1])
    above = jnp.concatenate([field[1:], empty], axis=0)
    below = jnp.concatenate([empty, field[:-1]], axis=0)
    return stiffness[:, None, None] * field + coupling * (2.0 * field - above - below)


def operate(padded, coef, stiffness):
    center = padded[:, 1:-1, 1:-1]
    beside = padded[:, 2:, 1:-1] + padded[:, :-2, 1:-1] + padded[:, 1:-1, 2:] + padded[:, 1:-1, :-2]
    return vertical(center, stiffness) + coef[None] * (4.0 * center - beside)


def coarsen(field):
    return 0.25 * (
        field[..., 0::2, 0::2]
        + field[..., 1::2, 0::2]
        + field[..., 0::2, 1::2]
        + field[..., 1::2, 1::2]
    )


def line_factors(stiffness):
    gain_in = jnp.sqrt(stiffness + 0.25 * stiffness * stiffness) - 0.5 * stiffness
    return (gain_in, 1.0 - gain_in)


def compose(earlier, later):
    return (earlier[0] * later[0], later[0][:, None] * earlier[1] + later[1])


def local(rhs, areas, stiffness):
    inverse = column_inverse(stiffness)

    def fine_residual(field):
        padded = extended(field, (("wide", 1), ("narrow", 2)), 1)
        return rhs - operate(padded, areas, stiffness)

    field = relaxation * apply_columns(inverse, rhs)
    field = field + relaxation * apply_columns(inverse, fine_residual(field))
    fine_res = fine_residual(field)
    coarse_rhs = coarsen(fine_res)
    coarse_coef = 0.25 * coarsen(areas)
    gain_in, retain = line_factors(stiffness)
    columns_x = coarse_rhs.shape[1]
    running = jnp.zeros_like(coarse_rhs[:, 0])
    forward_local = []
    for step in range(columns_x):
        running = gain_in[:, None] * coarse_rhs[:, step] + retain[:, None] * running
        forward_local.append(running)
    carried = retain**columns_x
    neutral = (jnp.ones_like(carried), jnp.zeros_like(running))
    _, entering = entering_2((carried, running), "wide", compose, neutral, False)
    forward = [
        forward_local[step] + (retain ** (step + 1))[:, None] * entering
        for step in range(columns_x)
    ]
    running = jnp.zeros_like(running)
    backward_local = [running] * columns_x
    for step in reversed(range(columns_x)):
        running = gain_in[:, None] * forward[step] + retain[:, None] * running
        backward_local[step] = running
    _, leaving = entering_2((carried, running), "wide", compose, neutral, True)
    backward = [
        backward_local[step] + (retain ** (columns_x - step))[:, None] * leaving
        for step in range(columns_x)
    ]
    line_corr = jnp.stack(backward, axis=1)
    coarse_pad = extended(line_corr, (("wide", 1), ("narrow", 2)), 1)
    coarse_corr = line_corr + relaxation * apply_columns(
        inverse, coarse_rhs - operate(coarse_pad, coarse_coef, stiffness)
    )
    field = field + jnp.repeat(jnp.repeat(coarse_corr, 2, axis=1), 2, axis=2)
    field = field + relaxation * apply_columns(inverse, fine_residual(field))
    field = field + relaxation * apply_columns(inverse, fine_residual(field))
    return (field, fine_residual(field))


def solution(mesh):
    placed = (P(None, "wide", "narrow"), P("wide", "narrow"), P())
    return jax.shard_map(
        local,
        mesh=mesh,
        in_specs=placed,
        out_specs=(P(None, "wide", "narrow"), P(None, "wide", "narrow")),
        check_vma=False,
    )
```

profile of v0, /device:TPU:20, one launch (start us, length us, event | category | flops | bytes accessed | tf_op | source)
XLA Modules:
  0.0 245.9 jit_solution(14019442602016105196)
XLA Ops:
  0.6 0.6 copy-done.4
  1.4 5.8 %cholesky.17 = f32[64,64]{1,0:T(8,128)S(1)} custom-call(f32[64,64]{1,0:T(8,128)S(1)} %add_multiply_fusion.1), custom_call_target="Cholesky" | custom-call | tf_op jit(solution)/shard_map/jit(cholesky)/cholesky | solution.py:52
  7.3 0.6 compare_reduce_fusion
  7.9 0.7 fusion.143
  8.6 4.9 %custom-call.6 = f32[1,64,64]{1,2,0:T(8,128)S(1)} custom-call(f32[1,64,64]{2,1,0:T(8,128)S(1)} %fusion.143), custom_call_target="InvertDiagBlocksLowerTriangular" | custom-call | tf_op jit(solution)/shard_map/triangular_solve | solution.py:53
  14.0 1.8 broadcast_multiply_fusion
  15.8 3.3 %collective-permute-start = (f32[64,1,256]{2,0,1:T(8,128)S(1)}, f32[64,1,256]{2,0,1:T(8,128)S(1)}, u32[]{:S(2)}, u32[]{:S(2)}) collective-permute-start(f32[64,1,256]{2,0,1:T(8,128)S(1)} %get-tuple-element.332), channel_id=1, source_target_pairs={{4,0},{8,4},{12,8},{16,12},{20,16},{24,20},{28,24},{5,1},{9,5},{13... | collective-permute-start | bytes 196616 | tf_op jit(solution)/shard_map/ppermute | solution.py:20
  19.0 2.6 %collective-permute-start.1 = (f32[64,1,256]{2,0,1:T(8,128)S(1)}, f32[64,1,256]{2,0,1:T(8,128)S(1)}, u32[]{:S(2)}, u32[]{:S(2)}) collective-permute-start(f32[64,1,256]{2,0,1:T(8,128)S(1)} %get-tuple-element.331), channel_id=1, source_target_pairs={{0,4},{4,8},{8,12},{12,16},{16,20},{20,24},{24,28},{1,5},{5,9},{9,... | collective-permute-start | bytes 196616 | tf_op jit(solution)/shard_map/ppermute | solution.py:18
  21.9 4.2 %collective-permute-done.1 = f32[64,1,256]{2,0,1:T(8,128)S(1)} collective-permute-done((f32[64,1,256]{2,0,1:T(8,128)S(1)}, f32[64,1,256]{2,0,1:T(8,128)S(1)}, u32[]{:S(2)}, u32[]{:S(2)}) %collective-permute-start.1) | collective-permute-done | bytes 65568 | tf_op jit(solution)/shard_map/ppermute | solution.py:18
  26.9 1.9 collective-permute-start.2
  28.8 3.2 %collective-permute-start.3 = (f32[64,10,1]{2,0,1:T(8,128)S(1)}, f32[64,10,1]{2,0,1:T(8,128)}, u32[]{:S(2)}, u32[]{:S(2)}) collective-permute-start(f32[64,10,1]{2,0,1:T(8,128)S(1)} %get-tuple-element.312), channel_id=1, source_target_pairs={{0,1},{1,2},{2,3},{4,5},{5,6},{6,7},{8,9},{9,10},{10,11},{12,13},{... | collective-permute-start | bytes 7688 | tf_op jit(solution)/shard_map/ppermute | solution.py:18
  32.7 0.6 dynamic-slice
  34.0 3.4 %collective-permute-done.3 = f32[64,10,1]{2,0,1:T(8,128)} collective-permute-done((f32[64,10,1]{2,0,1:T(8,128)S(1)}, f32[64,10,1]{2,0,1:T(8,128)}, u32[]{:S(2)}, u32[]{:S(2)}) %collective-permute-start.3) | collective-permute-done | bytes 2592 | tf_op jit(solution)/shard_map/ppermute | solution.py:18
  37.5 2.2 fusion.4
  39.7 1.9 collective-permute-start.4
  41.7 3.9 %collective-permute-start.5 = (f32[64,1,256]{2,0,1:T(8,128)S(1)}, f32[64,1,256]{2,0,1:T(8,128)S(1)}, u32[]{:S(2)}, u32[]{:S(2)}) collective-permute-start(f32[64,1,256]{2,0,1:T(8,128)S(1)} %get-tuple-element.327), channel_id=1, source_target_pairs={{0,4},{4,8},{8,12},{12,16},{16,20},{20,24},{24,28},{1,5},{5,9},{9,... | collective-permute-start | bytes 196616 | tf_op jit(solution)/shard_map/ppermute | solution.py:18
  46.6 14.6 %all-reduce.12 = f32[512]{0:T(512)S(1)} all-reduce(f32[512]{0:T(512)S(1)} %get-tuple-element.338), channel_id=2, replica_groups=mesh['wide'=8,'narrow'=4] {'wide'}, use_global_device_ids=true, to_apply=%add.12 | all-reduce | flops 512 | bytes 4096
  61.5 1.9 collective-permute-start.6
  63.4 2.4 collective-permute-start.7
  65.9 2.0 collective-permute-done.6
  68.0 3.8 %collective-permute-done.7 = f32[64,10,1]{2,0,1:T(8,128)S(1)} collective-permute-done((f32[64,10,1]{2,0,1:T(8,128)S(1)}, f32[64,10,1]{2,0,1:T(8,128)S(1)}, u32[]{:S(2)}, u32[]{:S(2)}) %collective-permute-start.7) | collective-permute-done | bytes 2592 | tf_op jit(solution)/shard_map/ppermute | solution.py:18
  71.8 0.6 fusion.45
  72.4 4.6 %slice.260 = f32[64,4,128]{2,0,1:T(8,128)S(1)} slice(f32[64,8,256]{2,0,1:T(8,128)S(1)} %fusion.45), slice={[0:64:1], [0:8:2], [0:256:2]} | slice | bytes 262144 | tf_op jit(solution)/shard_map/slice | solution.py:76
  77.1 4.7 %slice.261 = f32[64,4,128]{2,0,1:T(8,128)S(1)} slice(f32[64,8,256]{2,0,1:T(8,128)S(1)} %fusion.45), slice={[0:64:1], [1:8:2], [0:256:2]} | slice | bytes 262144 | tf_op jit(solution)/shard_map/slice | solution.py:77
  81.8 4.6 %slice.262 = f32[64,4,128]{2,0,1:T(8,128)S(1)} slice(f32[64,8,256]{2,0,1:T(8,128)S(1)} %fusion.45), slice={[0:64:1], [0:8:2], [1:256:2]} | slice | bytes 262144 | tf_op jit(solution)/shard_map/slice | solution.py:78
  86.5 4.7 %slice.263 = f32[64,4,128]{2,0,1:T(8,128)S(1)} slice(f32[64,8,256]{2,0,1:T(8,128)S(1)} %fusion.45), slice={[0:64:1], [1:8:2], [1:256:2]} | slice | bytes 262144 | tf_op jit(solution)/shard_map/slice | solution.py:79
  91.4 31.0 %all_gather.20 = f32[8,64,128]{2,1,0:T(8,128)S(1)} all-gather(f32[1,64,128]{2,1,0:T(8,128)S(1)} %fusion.156), channel_id=1, replica_groups=mesh['wide'=8,'narrow'=4] {'wide'}, dimensions={0}, use_global_device_ids=true | all-gather | bytes 294912 | tf_op jit(solution)/shard_map/all_gather | solution.py:29
  122.4 0.8 while.30
  123.3 30.8 %all-gather.1 = f32[512,128]{1,0:T(8,128)S(1)} all-gather(f32[64,128]{1,0:T(8,128)S(1)} %get-tuple-element.298), channel_id=3, replica_groups=mesh['wide'=8,'narrow'=4] {'wide'}, dimensions={0}, use_global_device_ids=true | all-gather | bytes 294912 | tf_op jit(solution)/shard_map/all_gather | solution.py:29
  154.1 0.8 while.31
  155.0 1.9 collective-permute-start.9
  157.0 4.8 %collective-permute-done.9 = f32[64,1,128]{2,0,1:T(8,128)S(1)} collective-permute-done((f32[64,1,128]{2,0,1:T(8,128)S(1)}, f32[64,1,128]{2,0,1:T(8,128)S(1)}, u32[]{:S(2)}, u32[]{:S(2)}) %collective-permute-start.9) | collective-permute-done | bytes 32800 | tf_op jit(solution)/shard_map/ppermute | solution.py:18
  162.0 2.8 %collective-permute-start.8 = (f32[64,1,128]{2,0,1:T(8,128)S(1)}, f32[64,1,128]{2,0,1:T(8,128)S(1)}, u32[]{:S(2)}, u32[]{:S(2)}) collective-permute-start(f32[64,1,128]{2,0,1:T(8,128)S(1)} %get-tuple-element.297), channel_id=1, source_target_pairs={{4,0},{8,4},{12,8},{16,12},{20,16},{24,20},{28,24},{5,1},{9,5},{13... | collective-permute-start | bytes 98312 | tf_op jit(solution)/shard_map/ppermute | solution.py:20
  164.8 3.0 %collective-permute-done.8 = f32[64,1,128]{2,0,1:T(8,128)S(1)} collective-permute-done((f32[64,1,128]{2,0,1:T(8,128)S(1)}, f32[64,1,128]{2,0,1:T(8,128)S(1)}, u32[]{:S(2)}, u32[]{:S(2)}) %collective-permute-start.8) | collective-permute-done | bytes 32800 | tf_op jit(solution)/shard_map/ppermute | solution.py:20
  167.9 1.9 collective-permute-start.10
  169.8 2.4 collective-permute-start.11
  172.3 0.7 collective-permute-done.10
  173.0 3.8 %collective-permute-done.11 = f32[64,6,1]{2,0,1:T(8,128)S(1)} collective-permute-done((f32[64,6,1]{2,0,1:T(8,128)S(1)}, f32[64,6,1]{2,0,1:T(8,128)S(1)}, u32[]{:S(2)}, u32[]{:S(2)}) %collective-permute-start.11) | collective-permute-done | bytes 1568 | tf_op jit(solution)/shard_map/ppermute | solution.py:18
  178.2 3.7 %collective-permute-start.12 = (f32[64,1,256]{2,0,1:T(8,128)S(1)}, f32[64,1,256]{2,0,1:T(8,128)S(1)}, u32[]{:S(2)}, u32[]{:S(2)}) collective-permute-start(f32[64,1,256]{2,0,1:T(8,128)S(1)} %get-tuple-element.324), channel_id=1, source_target_pairs={{4,0},{8,4},{12,8},{16,12},{20,16},{24,20},{28,24},{5,1},{9,5},{13... | collective-permute-start | bytes 196616 | tf_op jit(solution)/shard_map/ppermute | solution.py:20
  181.9 2.8 %collective-permute-start.13 = (f32[64,1,256]{2,0,1:T(8,128)S(1)}, f32[64,1,256]{2,0,1:T(8,128)S(1)}, u32[]{:S(2)}, u32[]{:S(2)}) collective-permute-start(f32[64,1,256]{2,0,1:T(8,128)S(1)} %get-tuple-element.323), channel_id=1, source_target_pairs={{0,4},{4,8},{8,12},{12,16},{16,20},{20,24},{24,28},{1,5},{5,9},{9,... | collective-permute-start | bytes 196616 | tf_op jit(solution)/shard_map/ppermute | solution.py:18
  185.2 3.7 %collective-permute-done.13 = f32[64,1,256]{2,0,1:T(8,128)S(1)} collective-permute-done((f32[64,1,256]{2,0,1:T(8,128)S(1)}, f32[64,1,256]{2,0,1:T(8,128)S(1)}, u32[]{:S(2)}, u32[]{:S(2)}) %collective-permute-start.13) | collective-permute-done | bytes 65568 | tf_op jit(solution)/shard_map/ppermute | solution.py:18
  189.2 1.9 collective-permute-start.14
  191.1 2.6 %collective-permute-start.15 = (f32[64,10,1]{2,0,1:T(8,128)S(1)}, f32[64,10,1]{2,0,1:T(8,128)S(1)}, u32[]{:S(2)}, u32[]{:S(2)}) collective-permute-start(f32[64,10,1]{2,0,1:T(8,128)S(1)} %get-tuple-element.308), channel_id=1, source_target_pairs={{0,1},{1,2},{2,3},{4,5},{5,6},{6,7},{8,9},{9,10},{10,11},{12,13},{... | collective-permute-start | bytes 7688 | tf_op jit(solution)/shard_map/ppermute | solution.py:18
  193.8 1.9 collective-permute-done.14
  195.7 4.0 %collective-permute-done.15 = f32[64,10,1]{2,0,1:T(8,128)S(1)} collective-permute-done((f32[64,10,1]{2,0,1:T(8,128)S(1)}, f32[64,10,1]{2,0,1:T(8,128)S(1)}, u32[]{:S(2)}, u32[]{:S(2)}) %collective-permute-start.15) | collective-permute-done | bytes 2592 | tf_op jit(solution)/shard_map/ppermute | solution.py:18
  199.7 1.2 fusion.3
  200.8 3.1 %collective-permute-start.16 = (f32[64,1,256]{2,0,1:T(8,128)S(1)}, f32[64,1,256]{2,0,1:T(8,128)S(1)}, u32[]{:S(2)}, u32[]{:S(2)}) collective-permute-start(f32[64,1,256]{2,0,1:T(8,128)S(1)} %get-tuple-element.320), channel_id=1, source_target_pairs={{4,0},{8,4},{12,8},{16,12},{20,16},{24,20},{28,24},{5,1},{9,5},{13... | collective-permute-start | bytes 196616 | tf_op jit(solution)/shard_map/ppermute | solution.py:20
  204.0 2.7 %collective-permute-start.17 = (f32[64,1,256]{2,0,1:T(8,128)S(1)}, f32[64,1,256]{2,0,1:T(8,128)S(1)}, u32[]{:S(2)}, u32[]{:S(2)}) collective-permute-start(f32[64,1,256]{2,0,1:T(8,128)S(1)} %get-tuple-element.319), channel_id=1, source_target_pairs={{0,4},{4,8},{8,12},{12,16},{16,20},{20,24},{24,28},{1,5},{5,9},{9,... | collective-permute-start | bytes 196616 | tf_op jit(solution)/shard_map/ppermute | solution.py:18
  207.0 4.0 %collective-permute-done.17 = f32[64,1,256]{2,0,1:T(8,128)S(1)} collective-permute-done((f32[64,1,256]{2,0,1:T(8,128)S(1)}, f32[64,1,256]{2,0,1:T(8,128)S(1)}, u32[]{:S(2)}, u32[]{:S(2)}) %collective-permute-start.17) | collective-permute-done | bytes 65568 | tf_op jit(solution)/shard_map/ppermute | solution.py:18
  211.2 1.9 collective-permute-start.18
  213.2 2.4 collective-permute-start.19
  215.7 2.0 collective-permute-done.18
  217.7 3.8 %collective-permute-done.19 = f32[64,10,1]{2,0,1:T(8,128)S(1)} collective-permute-done((f32[64,10,1]{2,0,1:T(8,128)S(1)}, f32[64,10,1]{2,0,1:T(8,128)S(1)}, u32[]{:S(2)}, u32[]{:S(2)}) %collective-permute-start.19) | collective-permute-done | bytes 2592 | tf_op jit(solution)/shard_map/ppermute | solution.py:18
  221.6 1.2 fusion.2
  222.8 3.9 %collective-permute-start.20 = (f32[64,1,256]{2,0,1:T(8,128)S(1)}, f32[64,1,256]{2,0,1:T(8,128)S(1)}, u32[]{:S(2)}, u32[]{:S(2)}) collective-permute-start(f32[64,1,256]{2,0,1:T(8,128)S(1)} %get-tuple-element.316), channel_id=1, source_target_pairs={{4,0},{8,4},{12,8},{16,12},{20,16},{24,20},{28,24},{5,1},{9,5},{13... | collective-permute-start | bytes 196616 | tf_op jit(solution)/shard_map/ppermute | solution.py:20
  226.7 1.9 collective-permute-start.21
  228.9 4.8 %collective-permute-done.21 = f32[64,1,256]{2,0,1:T(8,128)S(1)} collective-permute-done((f32[64,1,256]{2,0,1:T(8,128)S(1)}, f32[64,1,256]{2,0,1:T(8,128)S(1)}, u32[]{:S(2)}, u32[]{:S(2)}) %collective-permute-start.21) | collective-permute-done | bytes 65568 | tf_op jit(solution)/shard_map/ppermute | solution.py:18
  233.9 1.9 collective-permute-start.22
  235.9 2.4 collective-permute-start.23
  238.4 1.1 copy.31
  239.5 0.9 collective-permute-done.22
  240.4 3.8 %collective-permute-done.23 = f32[64,10,1]{2,0,1:T(8,128)S(1)} collective-permute-done((f32[64,10,1]{2,0,1:T(8,128)S(1)}, f32[64,10,1]{2,0,1:T(8,128)S(1)}, u32[]{:S(2)}, u32[]{:S(2)}) %collective-permute-start.23) | collective-permute-done | bytes 2592 | tf_op jit(solution)/shard_map/ppermute | solution.py:18
  244.3 0.6 fusion.10
  244.8 1.1 copy.32
  (105 shorter events, 9.2 us)
Async XLA Ops:
  0.6 0.7 copy-start.4
  15.8 6.2 %collective-permute-start = (f32[64,1,256]{2,0,1:T(8,128)S(1)}, f32[64,1,256]{2,0,1:T(8,128)S(1)}, u32[]{:S(2)}, u32[]{:S(2)}) collective-permute-start(f32[64,1,256]{2,0,1:T(8,128)S(1)} %get-tuple-element.332), channel_id=1, source_target_pairs={{4,0},{8,4},{12,8},{16,12},{20,16},{24,20},{28,24},{5,1},{9,5},{13... | collective-permute-start | bytes 196616 | tf_op jit(solution)/shard_map/ppermute | solution.py:20
  19.0 7.1 %collective-permute-start.1 = (f32[64,1,256]{2,0,1:T(8,128)S(1)}, f32[64,1,256]{2,0,1:T(8,128)S(1)}, u32[]{:S(2)}, u32[]{:S(2)}) collective-permute-start(f32[64,1,256]{2,0,1:T(8,128)S(1)} %get-tuple-element.331), channel_id=1, source_target_pairs={{0,4},{4,8},{8,12},{12,16},{16,20},{20,24},{24,28},{1,5},{5,9},{9,... | collective-permute-start | bytes 196616 | tf_op jit(solution)/shard_map/ppermute | solution.py:18
  21.9 4.2 %copy-start.2 = (f32[64,1,256]{2,0,1:T(8,128)}, f32[64,1,256]{2,0,1:T(8,128)S(1)}, u32[]{:S(2)}) copy-start(f32[64,1,256]{2,0,1:T(8,128)S(1)} %collective-permute-done) | copy-start | bytes 196612
  26.1 0.6 copy-start.3
  26.9 7.1 %collective-permute-start.2 = (f32[64,10,1]{2,0,1:T(8,128)S(1)}, f32[64,10,1]{2,0,1:T(8,128)}, u32[]{:S(2)}, u32[]{:S(2)}) collective-permute-start(f32[64,10,1]{2,0,1:T(8,128)S(1)} %get-tuple-element.311), channel_id=1, source_target_pairs={{1,0},{2,1},{3,2},{5,4},{6,5},{7,6},{9,8},{10,9},{11,10},{13,12},{... | collective-permute-start | bytes 7688 | tf_op jit(solution)/shard_map/ppermute | solution.py:20
  28.8 8.6 %copy-start = (f32[64,8,256]{2,1,0:T(8,128)S(1)}, f32[64,8,256]{2,1,0:T(8,128)}, u32[]{:S(2)}) copy-start(f32[64,8,256]{2,1,0:T(8,128)} %param.7) | copy-start | bytes 1572868
  28.8 8.6 %collective-permute-start.3 = (f32[64,10,1]{2,0,1:T(8,128)S(1)}, f32[64,10,1]{2,0,1:T(8,128)}, u32[]{:S(2)}, u32[]{:S(2)}) collective-permute-start(f32[64,10,1]{2,0,1:T(8,128)S(1)} %get-tuple-element.312), channel_id=1, source_target_pairs={{0,1},{1,2},{2,3},{4,5},{5,6},{6,7},{8,9},{9,10},{10,11},{12,13},{... | collective-permute-start | bytes 7688 | tf_op jit(solution)/shard_map/ppermute | solution.py:18
  32.1 0.7 copy-start.5
  32.2 5.3 %copy-start.1 = (f32[8,256]{1,0:T(8,128)S(1)}, f32[8,256]{1,0:T(8,128)}, u32[]{:S(2)}) copy-start(f32[8,256]{1,0:T(8,128)} %param.8) | copy-start | bytes 24580
  39.7 21.5 %collective-permute-start.4 = (f32[64,1,256]{2,0,1:T(8,128)S(1)}, f32[64,1,256]{2,0,1:T(8,128)S(1)}, u32[]{:S(2)}, u32[]{:S(2)}) collective-permute-start(f32[64,1,256]{2,0,1:T(8,128)S(1)} %get-tuple-element.328), channel_id=1, source_target_pairs={{4,0},{8,4},{12,8},{16,12},{20,16},{24,20},{28,24},{5,1},{9,5},{13... | collective-permute-start | bytes 196616 | tf_op jit(solution)/shard_map/ppermute | solution.py:20
  41.7 19.6 %collective-permute-start.5 = (f32[64,1,256]{2,0,1:T(8,128)S(1)}, f32[64,1,256]{2,0,1:T(8,128)S(1)}, u32[]{:S(2)}, u32[]{:S(2)}) collective-permute-start(f32[64,1,256]{2,0,1:T(8,128)S(1)} %get-tuple-element.327), channel_id=1, source_target_pairs={{0,4},{4,8},{8,12},{12,16},{16,20},{20,24},{24,28},{1,5},{5,9},{9,... | collective-permute-start | bytes 196616 | tf_op jit(solution)/shard_map/ppermute | solution.py:18
  61.5 6.5 %collective-permute-start.6 = (f32[64,10,1]{2,0,1:T(8,128)S(1)}, f32[64,10,1]{2,0,1:T(8,128)S(1)}, u32[]{:S(2)}, u32[]{:S(2)}) collective-permute-start(f32[64,10,1]{2,0,1:T(8,128)S(1)} %get-tuple-element.309), channel_id=1, source_target_pairs={{1,0},{2,1},{3,2},{5,4},{6,5},{7,6},{9,8},{10,9},{11,10},{13,12},{... | collective-permute-start | bytes 7688 | tf_op jit(solution)/shard_map/ppermute | solution.py:20
  63.4 8.4 %collective-permute-start.7 = (f32[64,10,1]{2,0,1:T(8,128)S(1)}, f32[64,10,1]{2,0,1:T(8,128)S(1)}, u32[]{:S(2)}, u32[]{:S(2)}) collective-permute-start(f32[64,10,1]{2,0,1:T(8,128)S(1)} %get-tuple-element.310), channel_id=1, source_target_pairs={{0,1},{1,2},{2,3},{4,5},{5,6},{6,7},{8,9},{9,10},{10,11},{12,13},{... | collective-permute-start | bytes 7688 | tf_op jit(solution)/shard_map/ppermute | solution.py:18
  155.0 6.7 %collective-permute-start.9 = (f32[64,1,128]{2,0,1:T(8,128)S(1)}, f32[64,1,128]{2,0,1:T(8,128)S(1)}, u32[]{:S(2)}, u32[]{:S(2)}) collective-permute-start(f32[64,1,128]{2,0,1:T(8,128)S(1)} %add_bitcast_fusion), channel_id=1, source_target_pairs={{0,4},{4,8},{8,12},{12,16},{16,20},{20,24},{24,28},{1,5},{5,9},{9,... | collective-permute-start | bytes 98312 | tf_op jit(solution)/shard_map/ppermute | solution.py:18
  162.0 5.8 %collective-permute-start.8 = (f32[64,1,128]{2,0,1:T(8,128)S(1)}, f32[64,1,128]{2,0,1:T(8,128)S(1)}, u32[]{:S(2)}, u32[]{:S(2)}) collective-permute-start(f32[64,1,128]{2,0,1:T(8,128)S(1)} %get-tuple-element.297), channel_id=1, source_target_pairs={{4,0},{8,4},{12,8},{16,12},{20,16},{24,20},{28,24},{5,1},{9,5},{13... | collective-permute-start | bytes 98312 | tf_op jit(solution)/shard_map/ppermute | solution.py:20
  167.9 5.1 %collective-permute-start.10 = (f32[64,6,1]{2,0,1:T(8,128)S(1)}, f32[64,6,1]{2,0,1:T(8,128)S(1)}, u32[]{:S(2)}, u32[]{:S(2)}) collective-permute-start(f32[64,6,1]{2,0,1:T(8,128)S(1)} %get-tuple-element.333), channel_id=1, source_target_pairs={{1,0},{2,1},{3,2},{5,4},{6,5},{7,6},{9,8},{10,9},{11,10},{13,12},{... | collective-permute-start | bytes 4616 | tf_op jit(solution)/shard_map/ppermute | solution.py:20
  169.8 7.0 %collective-permute-start.11 = (f32[64,6,1]{2,0,1:T(8,128)S(1)}, f32[64,6,1]{2,0,1:T(8,128)S(1)}, u32[]{:S(2)}, u32[]{:S(2)}) collective-permute-start(f32[64,6,1]{2,0,1:T(8,128)S(1)} %get-tuple-element.334), channel_id=1, source_target_pairs={{0,1},{1,2},{2,3},{4,5},{5,6},{6,7},{8,9},{9,10},{10,11},{12,13},{... | collective-permute-start | bytes 4616 | tf_op jit(solution)/shard_map/ppermute | solution.py:18
  178.2 7.1 %collective-permute-start.12 = (f32[64,1,256]{2,0,1:T(8,128)S(1)}, f32[64,1,256]{2,0,1:T(8,128)S(1)}, u32[]{:S(2)}, u32[]{:S(2)}) collective-permute-start(f32[64,1,256]{2,0,1:T(8,128)S(1)} %get-tuple-element.324), channel_id=1, source_target_pairs={{4,0},{8,4},{12,8},{16,12},{20,16},{24,20},{28,24},{5,1},{9,5},{13... | collective-permute-start | bytes 196616 | tf_op jit(solution)/shard_map/ppermute | solution.py:20
  181.9 7.1 %collective-permute-start.13 = (f32[64,1,256]{2,0,1:T(8,128)S(1)}, f32[64,1,256]{2,0,1:T(8,128)S(1)}, u32[]{:S(2)}, u32[]{:S(2)}) collective-permute-start(f32[64,1,256]{2,0,1:T(8,128)S(1)} %get-tuple-element.323), channel_id=1, source_target_pairs={{0,4},{4,8},{8,12},{12,16},{16,20},{20,24},{24,28},{1,5},{5,9},{9,... | collective-permute-start | bytes 196616 | tf_op jit(solution)/shard_map/ppermute | solution.py:18
  189.2 6.5 %collective-permute-start.14 = (f32[64,10,1]{2,0,1:T(8,128)S(1)}, f32[64,10,1]{2,0,1:T(8,128)S(1)}, u32[]{:S(2)}, u32[]{:S(2)}) collective-permute-start(f32[64,10,1]{2,0,1:T(8,128)S(1)} %get-tuple-element.307), channel_id=1, source_target_pairs={{1,0},{2,1},{3,2},{5,4},{6,5},{7,6},{9,8},{10,9},{11,10},{13,12},{... | collective-permute-start | bytes 7688 | tf_op jit(solution)/shard_map/ppermute | solution.py:20
  191.1 8.6 %collective-permute-start.15 = (f32[64,10,1]{2,0,1:T(8,128)S(1)}, f32[64,10,1]{2,0,1:T(8,128)S(1)}, u32[]{:S(2)}, u32[]{:S(2)}) collective-permute-start(f32[64,10,1]{2,0,1:T(8,128)S(1)} %get-tuple-element.308), channel_id=1, source_target_pairs={{0,1},{1,2},{2,3},{4,5},{5,6},{6,7},{8,9},{9,10},{10,11},{12,13},{... | collective-permute-start | bytes 7688 | tf_op jit(solution)/shard_map/ppermute | solution.py:18
  200.8 6.2 %collective-permute-start.16 = (f32[64,1,256]{2,0,1:T(8,128)S(1)}, f32[64,1,256]{2,0,1:T(8,128)S(1)}, u32[]{:S(2)}, u32[]{:S(2)}) collective-permute-start(f32[64,1,256]{2,0,1:T(8,128)S(1)} %get-tuple-element.320), channel_id=1, source_target_pairs={{4,0},{8,4},{12,8},{16,12},{20,16},{24,20},{28,24},{5,1},{9,5},{13... | collective-permute-start | bytes 196616 | tf_op jit(solution)/shard_map/ppermute | solution.py:20
  204.0 7.1 %collective-permute-start.17 = (f32[64,1,256]{2,0,1:T(8,128)S(1)}, f32[64,1,256]{2,0,1:T(8,128)S(1)}, u32[]{:S(2)}, u32[]{:S(2)}) collective-permute-start(f32[64,1,256]{2,0,1:T(8,128)S(1)} %get-tuple-element.319), channel_id=1, source_target_pairs={{0,4},{4,8},{8,12},{12,16},{16,20},{20,24},{24,28},{1,5},{5,9},{9,... | collective-permute-start | bytes 196616 | tf_op jit(solution)/shard_map/ppermute | solution.py:18
  211.2 6.5 %collective-permute-start.18 = (f32[64,10,1]{2,0,1:T(8,128)S(1)}, f32[64,10,1]{2,0,1:T(8,128)S(1)}, u32[]{:S(2)}, u32[]{:S(2)}) collective-permute-start(f32[64,10,1]{2,0,1:T(8,128)S(1)} %get-tuple-element.305), channel_id=1, source_target_pairs={{1,0},{2,1},{3,2},{5,4},{6,5},{7,6},{9,8},{10,9},{11,10},{13,12},{... | collective-permute-start | bytes 7688 | tf_op jit(solution)/shard_map/ppermute | solution.py:20
  213.2 8.4 %collective-permute-start.19 = (f32[64,10,1]{2,0,1:T(8,128)S(1)}, f32[64,10,1]{2,0,1:T(8,128)S(1)}, u32[]{:S(2)}, u32[]{:S(2)}) collective-permute-start(f32[64,10,1]{2,0,1:T(8,128)S(1)} %get-tuple-element.306), channel_id=1, source_target_pairs={{0,1},{1,2},{2,3},{4,5},{5,6},{6,7},{8,9},{9,10},{10,11},{12,13},{... | collective-permute-start | bytes 7688 | tf_op jit(solution)/shard_map/ppermute | solution.py:18
  222.8 6.2 %collective-permute-start.20 = (f32[64,1,256]{2,0,1:T(8,128)S(1)}, f32[64,1,256]{2,0,1:T(8,128)S(1)}, u32[]{:S(2)}, u32[]{:S(2)}) collective-permute-start(f32[64,1,256]{2,0,1:T(8,128)S(1)} %get-tuple-element.316), channel_id=1, source_target_pairs={{4,0},{8,4},{12,8},{16,12},{20,16},{24,20},{28,24},{5,1},{9,5},{13... | collective-permute-start | bytes 196616 | tf_op jit(solution)/shard_map/ppermute | solution.py:20
  226.7 7.1 %collective-permute-start.21 = (f32[64,1,256]{2,0,1:T(8,128)S(1)}, f32[64,1,256]{2,0,1:T(8,128)S(1)}, u32[]{:S(2)}, u32[]{:S(2)}) collective-permute-start(f32[64,1,256]{2,0,1:T(8,128)S(1)} %get-tuple-element.315), channel_id=1, source_target_pairs={{0,4},{4,8},{8,12},{12,16},{16,20},{20,24},{24,28},{1,5},{5,9},{9,... | collective-permute-start | bytes 196616 | tf_op jit(solution)/shard_map/ppermute | solution.py:18
  233.9 6.5 %collective-permute-start.22 = (f32[64,10,1]{2,0,1:T(8,128)S(1)}, f32[64,10,1]{2,0,1:T(8,128)S(1)}, u32[]{:S(2)}, u32[]{:S(2)}) collective-permute-start(f32[64,10,1]{2,0,1:T(8,128)S(1)} %get-tuple-element.303), channel_id=1, source_target_pairs={{1,0},{2,1},{3,2},{5,4},{6,5},{7,6},{9,8},{10,9},{11,10},{13,12},{... | collective-permute-start | bytes 7688 | tf_op jit(solution)/shard_map/ppermute | solution.py:20
  235.9 8.4 %collective-permute-start.23 = (f32[64,10,1]{2,0,1:T(8,128)S(1)}, f32[64,10,1]{2,0,1:T(8,128)S(1)}, u32[]{:S(2)}, u32[]{:S(2)}) collective-permute-start(f32[64,10,1]{2,0,1:T(8,128)S(1)} %get-tuple-element.304), channel_id=1, source_target_pairs={{0,1},{1,2},{2,3},{4,5},{5,6},{6,7},{8,9},{9,10},{10,11},{12,13},{... | collective-permute-start | bytes 7688 | tf_op jit(solution)/shard_map/ppermute | solution.py:18
where the time goes:
time: 247 us; the launch traced here: 246 us
  blocking collectives  76.5 us (31%)
  starting transfers between devices  61.6 us (25%)
  waiting for transfers between devices  56.2 us (23%)
  local copies, waits for them, and re-layouts  26.6 us (11%)
  other arithmetic  15.7 us (6%)
  matrix products  7.28 us (3%)
    all_gather x2, blocking collectives, entering_2(): everything = jax.tree.map(lambda part: lax.all_gather(part, axis), array)  61.9 us
    ppermute x12, waiting for transfers between devices, extended(): lax.ppermute(tail, axis, [(i, (i + 1) % count) for i in range(ends)])  44.2 us
    ppermute x12, starting transfers between devices, extended(): lax.ppermute(tail, axis, [(i, (i + 1) % count) for i in range(ends)])  31.4 us
    ppermute x12, starting transfers between devices, extended(): lax.ppermute(head, axis, [((i + 1) % count, i) for i in range(ends)])  30.2 us
    unnamed x1, blocking collectives  14.6 us
    ppermute x12, waiting for transfers between devices, extended(): lax.ppermute(head, axis, [((i + 1) % count, i) for i in range(ends)])  12.1 us
    dot_general x5, matrix products, apply_columns(): jnp.einsum('kl,lxy->kxy', inverse, field, precision=lax.Precision.HIGHEST)  6.82 us
    another operation x3, other arithmetic, column_inverse(): lower = jnp.linalg.cholesky(matrix)  6.52 us
  transfers between devices with their start and end apart: 24, of which 21 were waited for; matrix products, arithmetic and copies ran while one was open for 1% of the time, Pallas kernels for 0%

commit v1 on v0

v1 whole, which is shorter than its diff:
```python
import functools

import jax
import jax.numpy as jnp
from jax import lax
from jax.experimental import pallas as pl
from jax.experimental.pallas import tpu as pltpu
from jax.sharding import PartitionSpec as P

MESH = pl.DeviceIdType.MESH
f32 = jnp.float32
bf16 = jnp.bfloat16


def halves(value):
    high = value.astype(bf16)
    return high, (value - high.astype(f32)).astype(bf16)


def kernel(
    n_w, n_n, nx, ny, levels,
    rhs_ref, areas_ref, stiff_ref, p_out, r_out,
    fields, rhs_x, halo_x, pack_y, halo_y,
    line, line_hx, line_py, line_hy, scan_f, scan_z, scan_rf, scan_rz, theta, phi, stiff_b,
    send_sem, recv_sem, scan_send, scan_recv,
):
    cx, cy = nx // 2, ny // 2
    w, c = lax.axis_index("wide"), lax.axis_index("narrow")
    has = (w > 0, w < n_w - 1, c > 0, c < n_n - 1)
    to = (
        {"wide": jnp.maximum(w - 1, 0)},
        {"wide": jnp.minimum(w + 1, n_w - 1)},
        {"narrow": jnp.maximum(c - 1, 0)},
        {"narrow": jnp.minimum(c + 1, n_n - 1)},
    )
    strides = []
    while (1 << len(strides)) < n_w:
        strides.append(1 << len(strides))

    nothing = jnp.zeros((levels, ny), f32)
    small = nothing[:, :128]
    for side in range(2):
        @pl.when(jnp.logical_not(has[side]))
        def _():
            for stage in range(5):
                halo_x[stage, side] = nothing
            line_hx[side] = small

        @pl.when(jnp.logical_not(has[2 + side]))
        def _():
            for stage in range(5):
                halo_y[stage, side] = small
            line_hy[side] = small
    for i, s in enumerate(strides):
        @pl.when(w < s)
        def _():
            scan_rf[i] = small

        @pl.when(w >= n_w - s)
        def _():
            scan_rz[i] = small

    barrier = pltpu.get_barrier_semaphore()
    for side in range(4):
        @pl.when(has[side])
        def _():
            pl.semaphore_signal(barrier, inc=1, device_id=to[side], device_id_type=MESH)
    for s in strides[1:]:
        @pl.when(w >= s)
        def _():
            pl.semaphore_signal(
                barrier, inc=1, device_id={"wide": jnp.maximum(w - s, 0)}, device_id_type=MESH
            )

        @pl.when(w < n_w - s)
        def _():
            pl.semaphore_signal(
                barrier, inc=1, device_id={"wide": jnp.minimum(w + s, n_w - 1)}, device_id_type=MESH
            )

    before, now = jnp.float32(0.0), jnp.float32(1.0)
    for i in range(levels):
        theta[i : i + 1, :] = jnp.full((1, 128), now, f32)
        before, now = now, (stiff_ref[i] * 0.125 + 1.0) * now - 0.0625 * before
        stiff_b[i : i + 1, :] = jnp.full((1, 128), stiff_ref[i], f32)
    whole = jnp.full((levels, 128), now, f32)
    before, now = jnp.float32(0.0), jnp.float32(1.0)
    for i in reversed(range(levels)):
        phi[i : i + 1, :] = jnp.full((1, 128), now, f32)
        before, now = now, (stiff_ref[i] * 0.125 + 1.0) * now - 0.0625 * before
    row = lax.broadcasted_iota(jnp.int32, (levels, 128), 0)
    col = lax.broadcasted_iota(jnp.int32, (levels, 128), 1)
    apart = jnp.abs(row - col)
    decay = jnp.full((levels, 128), 0.4 * 0.125, f32)
    for b in range(6):
        decay = jnp.where((apart & (1 << b)) != 0, decay * (0.25 ** (1 << b)), decay)
    t_col, p_col = theta[...], phi[...]
    same = row == col
    t_row = jnp.sum(jnp.where(same, t_col, 0.0), axis=0, keepdims=True)
    p_row = jnp.sum(jnp.where(same, p_col, 0.0), axis=0, keepdims=True)
    inverse = (jnp.where(row <= col, t_col * p_row, p_col * t_row) * decay / whole)[:, :levels]
    inv_hi, inv_lo = halves(inverse)
    weights = jnp.concatenate([inv_hi, inv_hi, inv_lo], axis=1)

    def apply(value):
        high, low = halves(value)
        stacked = jnp.concatenate([high, low, high], axis=0)
        return jnp.dot(weights, stacked, preferred_element_type=f32)

    lane = lax.broadcasted_iota(jnp.int32, (levels, ny), 1)
    lane_c = lax.broadcasted_iota(jnp.int32, (levels, 128), 1)
    level = lax.broadcasted_iota(jnp.int32, (levels, ny), 0)

    def copies(stage):
        if stage < 5:
            sources = (fields.at[stage, 0], fields.at[stage, nx - 1], pack_y.at[stage, 0], pack_y.at[stage, 1])
            targets = (halo_x.at[stage, 1], halo_x.at[stage, 0], halo_y.at[stage, 1], halo_y.at[stage, 0])
        else:
            sources = (line.at[0], line.at[cx - 1], line_py.at[0], line_py.at[1])
            targets = (line_hx.at[1], line_hx.at[0], line_hy.at[1], line_hy.at[0])
        return [
            pltpu.make_async_remote_copy(
                src_ref=sources[i], dst_ref=targets[i], send_sem=send_sem.at[stage, i],
                recv_sem=recv_sem.at[stage, i], device_id=to[i], device_id_type=MESH,
            )
            for i in range(4)
        ]

    def start(stage, sides):
        every = copies(stage)
        for i in sides:
            @pl.when(has[i])
            def _():
                every[i].start()

    def arrive(stage):
        every = copies(stage)
        for i in range(4):
            @pl.when(has[i ^ 1])
            def _():
                every[i].wait_recv()

    def sent(stage):
        every = copies(stage)
        for i in range(4):
            @pl.when(has[i])
            def _():
                every[i].wait_send()

    order = (0, nx - 1) + tuple(range(1, nx - 1))

    def run(stage, compute):
        first = jnp.zeros((levels, 128), f32)
        last = jnp.zeros((levels, 128), f32)
        for at, x in enumerate(order):
            new = compute(x)
            fields[stage, x] = new
            if at == 1:
                start(stage, (0, 1))
            first = jnp.where(lane_c == x, pltpu.roll(new[:, :128], x, 1) if x else new[:, :128], first)
            last = jnp.where(lane_c == x, pltpu.roll(new[:, ny - 128 :], x + 1, 1), last)
        pack_y[stage, 0] = first
        pack_y[stage, 1] = last
        start(stage, (2, 3))

    def beside(stage, x):
        u = fields[stage, x]
        left = fields[stage, x - 1] if x else halo_x[stage, 0]
        right = fields[stage, x + 1] if x < nx - 1 else halo_x[stage, 1]
        low = halo_y[stage, 0]
        low = pltpu.roll(low, 128 - x, 1) if x else low
        high = pltpu.roll(halo_y[stage, 1], 127 - x, 1)
        edge = jnp.concatenate([low, high], axis=1)
        down = jnp.where(lane == 0, edge, pltpu.roll(u, 1, 1))
        up = jnp.where(lane == ny - 1, edge, pltpu.roll(u, ny - 1, 1))
        return u, left + right + down + up

    def smooth(stage, x):
        u, nb = beside(stage, x)
        a = areas_ref[x : x + 1, :]
        return 0.6 * u + apply(rhs_x[x] + (4.0 - 4.0 * a) * u + a * nb)

    def horizontal(stage, x):
        u, nb = beside(stage, x)
        a = areas_ref[x : x + 1, :]
        return u, rhs_x[x] - a * (4.0 * u - nb)

    def vertical(v):
        above = jnp.where(level == levels - 1, 0.0, pltpu.roll(v, levels - 1, 0))
        below = jnp.where(level == 0, 0.0, pltpu.roll(v, 1, 0))
        s = jnp.concatenate([stiff_b[...]] * (ny // 128), axis=1)
        return (s + 4.0) * v - 2.0 * (above + below)

    for x in range(nx):
        rhs_x[x] = rhs_ref[:, x, :]

    peers = sum(h.astype(jnp.int32) for h in has)
    for s in strides[1:]:
        peers = peers + (w >= s).astype(jnp.int32) + (w < n_w - s).astype(jnp.int32)
    pl.semaphore_wait(barrier, peers)

    run(0, lambda x: apply(rhs_x[x]))
    arrive(0)
    run(1, lambda x: smooth(0, x))

    s = stiff_b[...]
    keep = jnp.sqrt(s + 0.25 * s * s) - 0.5 * s
    r = 1.0 - keep
    power = [jnp.ones_like(r)]
    for _ in range(2 * cx + 1):
        power.append(power[-1] * r)
    tail = jnp.ones_like(r)
    base = power[2 * cx]
    for b in range(len(strides)):
        tail = jnp.where(((n_w - 1 - w) >> b) % 2 == 1, tail * base, tail)
        base = base * base
    scale = keep / (1.0 + r)
    pick = jnp.where(
        lax.broadcasted_iota(jnp.int32, (ny, cy), 0) // 2 == lax.broadcasted_iota(jnp.int32, (ny, cy), 1),
        1.0, 0.0,
    ).astype(bf16)
    spread = jnp.where(
        lax.broadcasted_iota(jnp.int32, (cy, ny), 1) // 2 == lax.broadcasted_iota(jnp.int32, (cy, ny), 0),
        1.0, 0.0,
    ).astype(bf16)

    def coarsen(pairs):
        rows = pairs.shape[0]
        high, low = halves(pairs)
        both = jnp.dot(jnp.concatenate([high, low], axis=0), pick, preferred_element_type=f32)
        return both[:rows] + both[rows:]

    pad_coef = [areas_ref[2 * x : 2 * x + 1, :] + areas_ref[2 * x + 1 : 2 * x + 2, :] for x in range(cx)]
    coef = [coarsen(jnp.broadcast_to(0.0625 * v, (16, ny)))[:1] for v in pad_coef]

    arrive(1)
    coarse = []
    for x in range(cx):
        u_a, h_a = horizontal(1, 2 * x)
        u_b, h_b = horizontal(1, 2 * x + 1)
        coarse.append(coarsen(0.25 * (h_a + h_b - vertical(u_a + u_b))))

    forward = coarse[0]
    for x in range(1, cx):
        forward = coarse[x] + r * forward
    backward = sum((power[x] - tail * power[2 * cx - x]) * coarse[x] for x in range(cx))
    enter = jnp.zeros_like(forward)
    leave = jnp.zeros_like(forward)
    step_all = power[cx]
    step_less = None
    for i, s in enumerate(strides):
        scan_f[i] = forward
        scan_z[i] = backward
        right = pltpu.make_async_remote_copy(
            src_ref=scan_f.at[i], dst_ref=scan_rf.at[i], send_sem=scan_send.at[i, 0], recv_sem=scan_recv.at[i, 0],
            device_id={"wide": jnp.minimum(w + s, n_w - 1)}, device_id_type=MESH,
        )
        left = pltpu.make_async_remote_copy(
            src_ref=scan_z.at[i], dst_ref=scan_rz.at[i], send_sem=scan_send.at[i, 1], recv_sem=scan_recv.at[i, 1],
            device_id={"wide": jnp.maximum(w - s, 0)}, device_id_type=MESH,
        )

        @pl.when(w < n_w - s)
        def _():
            right.start()

        @pl.when(w >= s)
        def _():
            left.start()

        @pl.when(w >= s)
        def _():
            right.wait_recv()

        @pl.when(w < n_w - s)
        def _():
            left.wait_recv()

        got_f, got_z = scan_rf[i], scan_rz[i]
        enter = enter + (got_f if step_less is None else step_less * got_f)
        leave = leave + (got_z if step_less is None else step_less * got_z)
        forward = forward + step_all * got_f
        backward = backward + step_all * got_z
        step_less = power[cx] if step_less is None else step_less * step_all
        step_all = step_all * step_all

        @pl.when(w < n_w - s)
        def _():
            right.wait_send()

        @pl.when(w >= s)
        def _():
            left.wait_send()

    first = jnp.zeros((levels, 128), f32)
    last = jnp.zeros((levels, 128), f32)
    for x in range(cx):
        total = (power[x + 1] - tail * power[2 * cx + 1 - x]) * enter + power[cx - x] * leave
        for j in range(cx):
            total = total + (power[abs(x - j)] - tail * power[2 * cx - x - j]) * coarse[j]
        total = scale * total
        line[x] = total
        first = jnp.where(lane_c == x, pltpu.roll(total, x, 1) if x else total, first)
        last = jnp.where(lane_c == x, pltpu.roll(total, x + 1, 1), last)
    line_py[0] = first
    line_py[1] = last
    start(5, range(4))
    arrive(5)

    def correction(x):
        v = line[x]
        left = line[x - 1] if x else line_hx[0]
        right = line[x + 1] if x < cx - 1 else line_hx[1]
        low = pltpu.roll(line_hy[0], 128 - x, 1) if x else line_hy[0]
        high = pltpu.roll(line_hy[1], 127 - x, 1)
        down = jnp.where(lane_c == 0, low, pltpu.roll(v, 1, 1))
        up = jnp.where(lane_c == cy - 1, high, pltpu.roll(v, cy - 1, 1))
        a = coef[x]
        value = 0.6 * v + apply(coarse[x] + (4.0 - 4.0 * a) * v + a * (left + right + down + up))
        high, low = halves(value)
        both = jnp.dot(jnp.concatenate([high, low], axis=0), spread, preferred_element_type=f32)
        return both[:levels] + both[levels:]

    corrections = {}

    def corrected(x):
        if x // 2 not in corrections:
            corrections[x // 2] = correction(x // 2)
        return fields[1, x] + corrections[x // 2]

    run(2, corrected)
    arrive(2)
    run(3, lambda x: smooth(2, x))
    arrive(3)
    run(4, lambda x: smooth(3, x))
    for x in range(nx):
        p_out[:, x, :] = fields[4, x]
    arrive(4)
    for x in range(nx):
        u, h = horizontal(4, x)
        r_out[:, x, :] = h - vertical(u)
    for stage in range(6):
        sent(stage)


def local(n_w, n_n, rhs, areas, stiffness):
    levels, nx, ny = rhs.shape
    cx = nx // 2
    steps = max(1, (n_w - 1).bit_length())
    vmem = lambda *shape: pltpu.VMEM(shape, f32)
    whole = pl.BlockSpec(memory_space=pltpu.VMEM)
    return pl.pallas_call(
        functools.partial(kernel, n_w, n_n, nx, ny, levels),
        out_shape=[jax.ShapeDtypeStruct(rhs.shape, f32)] * 2,
        in_specs=[whole, whole, pl.BlockSpec(memory_space=pltpu.SMEM)],
        out_specs=[whole, whole],
        scratch_shapes=[
            vmem(5, nx, levels, ny), vmem(nx, levels, ny), vmem(5, 2, levels, ny),
            vmem(5, 2, levels, 128), vmem(5, 2, levels, 128),
            vmem(cx, levels, 128), vmem(2, levels, 128), vmem(2, levels, 128), vmem(2, levels, 128),
            vmem(steps, levels, 128), vmem(steps, levels, 128),
            vmem(steps, levels, 128), vmem(steps, levels, 128),
            vmem(levels, 128), vmem(levels, 128), vmem(levels, 128),
            pltpu.SemaphoreType.DMA((6, 4)), pltpu.SemaphoreType.DMA((6, 4)),
            pltpu.SemaphoreType.DMA((steps, 2)), pltpu.SemaphoreType.DMA((steps, 2)),
        ],
        compiler_params=pltpu.CompilerParams(
            collective_id=0, has_side_effects=True, vmem_limit_bytes=40 * 1024 * 1024
        ),
        cost_estimate=pl.CostEstimate(flops=80_000_000, bytes_accessed=1_600_000, transcendentals=0),
    )(rhs, areas, stiffness)


def solution(mesh):
    placed = (P(None, "wide", "narrow"), P("wide", "narrow"), P())
    return jax.shard_map(
        functools.partial(local, mesh.shape["wide"], mesh.shape["narrow"]),
        mesh=mesh,
        in_specs=placed,
        out_specs=(P(None, "wide", "narrow"), P(None, "wide", "narrow")),
        check_vma=False,
    )
```

time: 247 us -> 46.8 us (0.19)
  the two profiles are of different devices: /device:TPU:20 before, /device:TPU:0 now
where the time goes in v1:
time: 46.8 us; the launch traced here: 46.6 us
  Pallas kernels  42 us (90%)
  local copies, waits for them, and re-layouts  3.97 us (8%)
  between operations  0.65 us (1%)
    pallas_call x1, Pallas kernels, local(): pl.pallas_call(functools.partial(kernel, n_w, n_n, nx, ny, levels), out_s...  42 us
    unnamed x8, local copies, waits for them, and re-layouts  3.97 us

profile of v1, /device:TPU:0, one launch (start us, length us, event | category | flops | bytes accessed | tf_op | source)
XLA Modules:
  0.0 46.6 jit_solution(9112915825407617064)
XLA Ops:
  0.6 0.0 copy-start
  0.6 1.0 %copy-done = f32[64,8,256]{2,1,0:T(8,128)S(1)} copy-done((f32[64,8,256]{2,1,0:T(8,128)S(1)}, f32[64,8,256]{2,1,0:T(8,128)}, u32[]{:S(2)}) %copy-start) | copy-done | bytes 524312
  1.7 0.0 copy-start.1
  1.7 0.7 %copy-done.1 = f32[8,256]{1,0:T(8,128)S(1)} copy-done((f32[8,256]{1,0:T(8,128)S(1)}, f32[8,256]{1,0:T(8,128)}, u32[]{:S(2)}) %copy-start.1) | copy-done | bytes 8216
  2.4 0.0 copy-start.2
  2.4 0.7 %copy-done.2 = f32[64]{0:T(128)S(1)} copy-done((f32[64]{0:T(128)S(1)}, f32[64]{0:T(128)}, u32[]{:S(2)}) %copy-start.2) | copy-done | bytes 280
  3.0 42.0 %shard_map.50 = (f32[64,8,256]{2,1,0:T(8,128)S(1)}, f32[64,8,256]{2,1,0:T(8,128)S(1)}) custom-call(f32[64,8,256]{2,1,0:T(8,128)S(1)} %copy-done, f32[8,256]{1,0:T(8,128)S(1)} %copy-done.1, f32[64]{0:T(128)S(1)} %copy-done.2), custom_call_target="tpu_custom_call" | custom-call | flops 80000000 | bytes 1600000 | tf_op jit(solution)/shard_map/pallas_call | solution.py:352
  45.0 0.8 %copy.7 = f32[64,8,256]{2,1,0:T(8,128)} copy(f32[64,8,256]{2,1,0:T(8,128)S(1)} %get-tuple-element.4) | data formatting | bytes 1048576
  45.8 0.8 %copy.8 = f32[64,8,256]{2,1,0:T(8,128)} copy(f32[64,8,256]{2,1,0:T(8,128)S(1)} %get-tuple-element.5) | data formatting | bytes 1048576
Async XLA Ops:
  0.6 1.0 %copy-start = (f32[64,8,256]{2,1,0:T(8,128)S(1)}, f32[64,8,256]{2,1,0:T(8,128)}, u32[]{:S(2)}) copy-start(f32[64,8,256]{2,1,0:T(8,128)} %rhs_ref.1) | copy-start | bytes 1572868
  1.7 0.7 %copy-start.1 = (f32[8,256]{1,0:T(8,128)S(1)}, f32[8,256]{1,0:T(8,128)}, u32[]{:S(2)}) copy-start(f32[8,256]{1,0:T(8,128)} %areas_ref.1) | copy-start | bytes 24580
  2.4 0.7 %copy-start.2 = (f32[64]{0:T(128)S(1)}, f32[64]{0:T(128)}, u32[]{:S(2)}) copy-start(f32[64]{0:T(128)} %stiff_ref.1) | copy-start | bytes 772

commit v2 on v1

v2 whole, which is shorter than its diff:
```python
import functools

import jax
import jax.numpy as jnp
from jax import lax
from jax.experimental import pallas as pl
from jax.experimental.pallas import tpu as pltpu
from jax.sharding import PartitionSpec as P

MESH = pl.DeviceIdType.MESH
f32 = jnp.float32
bf16 = jnp.bfloat16


def halves(value):
    high = value.astype(bf16)
    return high, (value - high.astype(f32)).astype(bf16)


def kernel(
    n_w, n_n, nx, ny, levels,
    rhs_ref, areas_ref, stiff_ref, p_out, r_out,
    rhs_x, u1, u2, u3, u4, p, wide_a, coarse, line, pack, strip, corner, pack_a, strip_a,
    scan_f, scan_z, scan_rf, scan_rz, theta, phi, stiff_b,
    send_sem, recv_sem, scan_send, scan_recv,
):
    cx, cy = nx // 2, ny // 2
    w, c = lax.axis_index("wide"), lax.axis_index("narrow")
    has = (w > 0, w < n_w - 1, c > 0, c < n_n - 1)
    to = (
        {"wide": jnp.maximum(w - 1, 0)},
        {"wide": jnp.minimum(w + 1, n_w - 1)},
        {"narrow": jnp.maximum(c - 1, 0)},
        {"narrow": jnp.minimum(c + 1, n_n - 1)},
    )
    strides = []
    while (1 << len(strides)) < n_w:
        strides.append(1 << len(strides))
    own = 3

    small = jnp.zeros((levels, 128), f32)
    nothing = jnp.zeros((levels, ny), f32)
    edge_x = (
        ((1, 2), (0, 1), (0, 1, 2, 3)),
        ((nx + 3, nx + 4), (nx + 4, nx + 5), (cx + 4, cx + 5, cx + 6, cx + 7)),
    )
    rhs_x[0] = nothing
    rhs_x[nx + 5] = nothing
    for side in range(2):
        @pl.when(jnp.logical_not(has[side]))
        def _():
            for e in edge_x[side][0]:
                rhs_x[e] = nothing
            for e in edge_x[side][1]:
                u2[e] = nothing
            for e in edge_x[side][2]:
                coarse[e] = small
            corner[0, side] = small
            corner[1, side] = small
            wide_a[2 * side * nx : 2 * side * nx + nx, :] = jnp.zeros((nx, ny), f32)

        @pl.when(jnp.logical_not(has[2 + side]))
        def _():
            strip[side] = small
            strip[2 + 2 * side] = small
            strip[3 + 2 * side] = small
            strip_a[side] = jnp.zeros((16, 128), f32)
    for i, s in enumerate(strides):
        @pl.when(w < s)
        def _():
            scan_rf[i] = small

        @pl.when(w >= n_w - s)
        def _():
            scan_rz[i] = small

    barrier = pltpu.get_barrier_semaphore()
    for side in range(4):
        @pl.when(has[side])
        def _():
            pl.semaphore_signal(barrier, inc=1, device_id=to[side], device_id_type=MESH)
    for s in strides[1:]:
        @pl.when(w >= s)
        def _():
            pl.semaphore_signal(
                barrier, inc=1, device_id={"wide": jnp.maximum(w - s, 0)}, device_id_type=MESH
            )

        @pl.when(w < n_w - s)
        def _():
            pl.semaphore_signal(
                barrier, inc=1, device_id={"wide": jnp.minimum(w + s, n_w - 1)}, device_id_type=MESH
            )

    exchanges = {
        "areas": (0, (wide_a.at[pl.ds(nx, nx)], wide_a.at[pl.ds(2 * nx, nx)]),
                  (wide_a.at[pl.ds(nx, nx)], wide_a.at[pl.ds(0, nx)])),
        "rhs": (0, (rhs_x.at[pl.ds(own, 2)], rhs_x.at[pl.ds(own + nx, 2)]),
                (rhs_x.at[pl.ds(own + nx - 2, 2)], rhs_x.at[pl.ds(own - 2, 2)])),
        "corner": (0, (pack.at[1], corner.at[0, 1]), (pack.at[1], corner.at[0, 0])),
        "u2": (0, (u2.at[pl.ds(own + 1, 2)], u2.at[pl.ds(own + nx + 1, 2)]),
               (u2.at[pl.ds(own + nx - 3, 2)], u2.at[pl.ds(own - 3, 2)])),
        "u2corner": (0, (pack.at[2], corner.at[1, 1]), (pack.at[2], corner.at[1, 0])),
        "coarse": (0, (coarse.at[pl.ds(4, cx)], coarse.at[pl.ds(4 + cx, cx)]),
                   (coarse.at[pl.ds(4, cx)], coarse.at[pl.ds(4 - cx, cx)])),
        "strip": (1, (pack.at[0], strip.at[1]), (pack.at[0], strip.at[0])),
        "strip_a": (1, (pack_a, strip_a.at[1]), (pack_a, strip_a.at[0])),
        "line": (1, (pack.at[pl.ds(3, 2)], strip.at[pl.ds(4, 2)]), (pack.at[pl.ds(3, 2)], strip.at[pl.ds(2, 2)])),
    }
    names = list(exchanges)

    def copies(name):
        axis, low, high = exchanges[name]
        at = names.index(name)
        return [
            (
                pltpu.make_async_remote_copy(
                    src_ref=pair[0], dst_ref=pair[1], send_sem=send_sem.at[at, i], recv_sem=recv_sem.at[at, i],
                    device_id=to[2 * axis + i], device_id_type=MESH,
                ),
                has[2 * axis + i],
                has[2 * axis + 1 - i],
            )
            for i, pair in enumerate((low, high))
        ]

    def start(name):
        for copy, goes, _ in copies(name):
            @pl.when(goes)
            def _():
                copy.start()

    def arrive(*which):
        for name in which:
            for copy, _, comes in copies(name):
                @pl.when(comes)
                def _():
                    copy.wait_recv()

    lane = lax.broadcasted_iota(jnp.int32, (levels, ny), 1)
    lane_c = lax.broadcasted_iota(jnp.int32, (levels, 128), 1)
    level = lax.broadcasted_iota(jnp.int32, (levels, ny), 0)
    inner = lane_c % 8 < 4
    row_c = lane_c // 8

    def packed(rows, base=None):
        result = jnp.zeros((levels, 128), f32) if base is None else base
        for e, value in rows:
            ends = jnp.where(lane_c < 4, value[:, :128], value[:, value.shape[1] - 128 :])
            result = jnp.where(row_c == e, pltpu.roll(ends, 8 * e + 4, 1), result)
        return result

    def strips(mine, low, high):
        return jnp.concatenate([jnp.where(inner, low, mine), jnp.where(inner, mine, high)], axis=1)

    wide_a[nx : 2 * nx, :] = areas_ref[...]
    for x in (0, 1, nx - 2, nx - 1) + tuple(range(2, nx - 2)):
        rhs_x[own + x] = rhs_ref[:, x, :]
    peers = sum(h.astype(jnp.int32) for h in has)
    for s in strides[1:]:
        peers = peers + (w >= s).astype(jnp.int32) + (w < n_w - s).astype(jnp.int32)
    pl.semaphore_wait(barrier, peers)
    start("areas")
    start("rhs")
    pack_rhs = packed([(e, rhs_x[e]) for e in range(own, own + nx)])
    pack[0] = pack_rhs
    start("strip")

    before, now = jnp.float32(0.0), jnp.float32(1.0)
    for i in range(levels):
        theta[i : i + 1, :] = jnp.full((1, 128), now, f32)
        before, now = now, (stiff_ref[i] * 0.125 + 1.0) * now - 0.0625 * before
        stiff_b[i : i + 1, :] = jnp.full((1, 128), stiff_ref[i], f32)
    whole = jnp.full((levels, 128), now, f32)
    before, now = jnp.float32(0.0), jnp.float32(1.0)
    for i in reversed(range(levels)):
        phi[i : i + 1, :] = jnp.full((1, 128), now, f32)
        before, now = now, (stiff_ref[i] * 0.125 + 1.0) * now - 0.0625 * before
    row = lax.broadcasted_iota(jnp.int32, (levels, 128), 0)
    col = lax.broadcasted_iota(jnp.int32, (levels, 128), 1)
    apart = jnp.abs(row - col)
    decay = jnp.full((levels, 128), 0.4 * 0.125, f32)
    for b in range(6):
        decay = jnp.where((apart & (1 << b)) != 0, decay * (0.25 ** (1 << b)), decay)
    t_col, p_col = theta[...], phi[...]
    same = row == col
    t_row = jnp.sum(jnp.where(same, t_col, 0.0), axis=0, keepdims=True)
    p_row = jnp.sum(jnp.where(same, p_col, 0.0), axis=0, keepdims=True)
    inverse = (jnp.where(row <= col, t_col * p_row, p_col * t_row) * decay / whole)[:, :levels]
    inv_hi, inv_lo = halves(inverse)
    weights = jnp.concatenate([inv_hi, inv_hi, inv_lo], axis=1)

    def apply(value):
        high, low = halves(value)
        stacked = jnp.concatenate([high, low, high], axis=0)
        return jnp.dot(weights, stacked, preferred_element_type=f32)

    def area(e):
        return wide_a[nx + e - own : nx + e - own + 1, :]

    def sides(u, sides_of, e):
        n = u.shape[1]
        index = lane[:, :n]
        low = pltpu.roll(sides_of[:, :128], (125 - 8 * e) % 128, 1)
        high = pltpu.roll(sides_of[:, 128:], (123 - 8 * e) % 128, 1)
        if n == 128:
            down = jnp.where(index == 0, low, pltpu.roll(u, 1, 1))
            return down + jnp.where(index == n - 1, high, pltpu.roll(u, n - 1, 1))
        edge = jnp.concatenate([low, high], axis=1)
        down = jnp.where(index == 0, edge, pltpu.roll(u, 1, 1))
        return down + jnp.where(index == n - 1, edge, pltpu.roll(u, n - 1, 1))

    def smooth(field, sides_of, e):
        u = field[e]
        nb = field[e - 1] + field[e + 1] + sides(u, sides_of, e)
        a = area(e)
        return 0.6 * u + apply(rhs_x[e] + (4.0 - 4.0 * a) * u + a * nb)

    def smooth_strip(s, right_side, a):
        nb = pltpu.roll(s, 1, 1) + pltpu.roll(s, ny - 1, 1) + pltpu.roll(s, 8, 1) + pltpu.roll(s, ny - 8, 1)
        return 0.6 * s + apply(right_side + (4.0 - 4.0 * a) * s + a * nb)

    def horizontal(field, sides_of, e):
        u = field[e]
        nb = field[e - 1] + field[e + 1] + sides(u, sides_of, e)
        return u, rhs_x[e] - area(e) * (4.0 * u - nb)

    def vertical(v):
        above = jnp.where(level == levels - 1, 0.0, pltpu.roll(v, levels - 1, 0))
        below = jnp.where(level == 0, 0.0, pltpu.roll(v, 1, 0))
        s = jnp.concatenate([stiff_b[...]] * (ny // 128), axis=1)
        return (s + 4.0) * v - 2.0 * (above + below)

    pick = jnp.where(
        lax.broadcasted_iota(jnp.int32, (ny, cy), 0) // 2 == lax.broadcasted_iota(jnp.int32, (ny, cy), 1),
        1.0, 0.0,
    ).astype(bf16)
    spread = jnp.where(
        lax.broadcasted_iota(jnp.int32, (cy, ny), 1) // 2 == lax.broadcasted_iota(jnp.int32, (cy, ny), 0),
        1.0, 0.0,
    ).astype(bf16)
    fine_lane = lax.broadcasted_iota(jnp.int32, (128, 128), 1)
    spread_strip = jnp.where(
        lax.broadcasted_iota(jnp.int32, (128, 128), 0)
        == 8 * ((fine_lane // 8 + 3) // 2) + 2 + (fine_lane % 8) // 2,
        1.0, 0.0,
    ).astype(bf16)

    def exact(value, matrix):
        rows = value.shape[0]
        high, low = halves(value)
        both = jnp.dot(jnp.concatenate([high, low], axis=0), matrix, preferred_element_type=f32)
        return both[:rows] + both[rows:]

    for e in range(own, own + nx):
        u1[e] = apply(rhs_x[e])

    arrive("strip")
    halo = jnp.where(inner, strip[0], strip[1])
    pack[1] = halo
    start("corner")
    first = apply(strips(pack_rhs, halo, halo))
    for e in range(own + 1, own + nx - 1):
        u2[e] = smooth(u1, first, e)

    arrive("areas")
    eight = lane_c[:8]
    packed_a = jnp.zeros((8, 128), f32)
    for e in range(0, nx + 6):
        v = jnp.broadcast_to(area(e), (8, ny))
        v = pltpu.roll(jnp.where(eight < 4, v[:, :128], v[:, ny - 128 :]), 8 * e + 4, 1)
        packed_a = jnp.where(eight // 8 == e, v, packed_a)
    sums = []
    for x in range(-2, cx + 2):
        at = nx + 2 * x
        sums.append(jnp.broadcast_to(0.0625 * (wide_a[at : at + 1, :] + wide_a[at + 1 : at + 2, :]), (8, ny)))
    coef = exact(jnp.concatenate(sums, axis=0), pick)
    coef = {x: coef[8 * (x + 2) : 8 * (x + 2) + 8] for x in range(-2, cx + 2)}
    packed_c = jnp.zeros((8, 128), f32)
    for x in range(-2, cx + 2):
        v = pltpu.roll(coef[x], 8 * (x + 3) + 4, 1)
        packed_c = jnp.where(eight // 8 == x + 3, v, packed_c)
    pack_a[0:8, :] = packed_a
    pack_a[8:16, :] = packed_c
    start("strip_a")

    arrive("rhs")
    outer = (own - 2, own - 1, own + nx, own + nx + 1)
    for e in outer:
        u1[e] = apply(rhs_x[e])
    pack_all = packed([(e, rhs_x[e]) for e in outer], pack_rhs)
    arrive("corner", "strip_a")
    halo = jnp.where(
        row_c < own, pltpu.roll(corner[0, 0], 64, 1),
        jnp.where(row_c >= own + nx, pltpu.roll(corner[0, 1], 64, 1), halo),
    )
    rhs_strip = strips(pack_all, halo, halo)
    inner_a = eight % 8 < 4

    def strips_a(low, high, mine):
        return jnp.concatenate([jnp.where(inner_a, low, mine), jnp.where(inner_a, mine, high)], axis=1)[:1]

    a_strip = strips_a(strip_a[0, 0:8, :], strip_a[1, 0:8, :], packed_a)
    c_strip = strips_a(strip_a[0, 8:16, :], strip_a[1, 8:16, :], packed_c)
    first = apply(rhs_strip)
    for e in (own - 1, own, own + nx - 1, own + nx):
        u2[e] = smooth(u1, first, e)
    second = smooth_strip(first, rhs_strip, a_strip)

    s = stiff_b[...]
    keep = jnp.sqrt(s + 0.25 * s * s) - 0.5 * s
    r = 1.0 - keep
    power = [jnp.ones_like(r)]
    for _ in range(4 * cx):
        power.append(power[-1] * r)
    is_last = w == n_w - 1
    far = jnp.ones_like(r)
    base = power[2 * cx]
    steps = jnp.maximum(n_w - 2 - w, 0)
    for b in range(len(strides)):
        far = jnp.where((steps >> b) % 2 == 1, far * base, far)
        base = base * base
    tail = jnp.where(is_last, power[0], far * power[2 * cx])
    scale = keep / (1.0 + r)

    for x in range(cx):
        e = own + 2 * x
        u_a, h_a = horizontal(u2, second, e)
        u_b, h_b = horizontal(u2, second, e + 1)
        coarse[4 + x] = exact(0.25 * (h_a + h_b - vertical(u_a + u_b)), pick)
    mine = [coarse[4 + x] for x in range(cx)]
    forward = mine[0]
    for x in range(1, cx):
        forward = mine[x] + r * forward
    backward = sum((power[x] - tail * power[2 * cx - x]) * mine[x] for x in range(cx))
    enter = jnp.zeros_like(forward)
    leave = jnp.zeros_like(forward)
    step_all = power[cx]
    step_less = None
    scans = []
    for i, s in enumerate(strides):
        scan_f[i] = forward
        scan_z[i] = backward
        right = pltpu.make_async_remote_copy(
            src_ref=scan_f.at[i], dst_ref=scan_rf.at[i], send_sem=scan_send.at[i, 0], recv_sem=scan_recv.at[i, 0],
            device_id={"wide": jnp.minimum(w + s, n_w - 1)}, device_id_type=MESH,
        )
        left = pltpu.make_async_remote_copy(
            src_ref=scan_z.at[i], dst_ref=scan_rz.at[i], send_sem=scan_send.at[i, 1], recv_sem=scan_recv.at[i, 1],
            device_id={"wide": jnp.maximum(w - s, 0)}, device_id_type=MESH,
        )
        scans.append((right, left, s))

        @pl.when(w < n_w - s)
        def _():
            right.start()

        @pl.when(w >= s)
        def _():
            left.start()

        if i == 0:
            start("coarse")
            start("u2")
            pack[2] = jnp.where(inner, second[:, :128], second[:, 128:])
            start("u2corner")

        @pl.when(w >= s)
        def _():
            right.wait_recv()

        @pl.when(w < n_w - s)
        def _():
            left.wait_recv()

        got_f, got_z = scan_rf[i], scan_rz[i]
        forward = forward + step_all * got_f
        backward = backward + step_all * got_z
        if i:
            enter = enter + (got_f if i == 1 else step_less * got_f)
            leave = leave + (got_z if i == 1 else step_less * got_z)
            step_less = step_all if i == 1 else step_less * step_all
        step_all = step_all * step_all

    arrive("coarse")
    window = range(-4, cx + 4)
    causal = {-5: enter}
    beyond = {cx + 3: r * leave}
    total = enter * jnp.where(is_last, power[2 * cx + 2], far * power[2 * cx + 6])
    for t in window:
        value = coarse[4 + t]
        causal[t] = value + r * causal[t - 1]
        total = total + value * jnp.where(is_last, power[max(cx + 1 - t, 0)], far * power[2 * cx + 1 - t])
    for t in reversed(range(-4, cx + 3)):
        beyond[t] = r * (beyond[t + 1] + coarse[4 + t + 1])
    for t in range(-3, cx + 3):
        back = jnp.where(is_last, power[max(cx - 1 - t, 0)], power[cx + 3 - t])
        value = scale * (causal[t] + beyond[t] - back * total)
        if t < 0:
            value = jnp.where(w == 0, 0.0, value)
        if t >= cx:
            value = jnp.where(is_last, 0.0, value)
        line[4 + t] = value
    pack_c = packed([(t + 3, coarse[4 + t]) for t in range(-3, cx + 3)])
    pack_l = packed([(t + 3, line[4 + t]) for t in range(-3, cx + 3)])
    pack[3] = pack_c
    pack[4] = pack_l
    start("line")

    arrive("u2", "u2corner")
    halo = jnp.where(
        row_c < own - 1, pltpu.roll(corner[1, 0], 64, 1),
        jnp.where(row_c > own + nx, pltpu.roll(corner[1, 1], 64, 1), pack[2]),
    )
    second = strips(packed([(e, u2[e]) for e in range(nx + 6)]), halo, halo)

    arrive("line")
    c_sides = strips(pack_c, strip[2], strip[4])
    l_sides = strips(pack_l, strip[3], strip[5])

    def correction(x):
        v = line[4 + x]
        nb = line[3 + x] + line[5 + x] + sides(v, l_sides, x + 3)
        a = coef[x][:1]
        return exact(0.6 * v + apply(coarse[4 + x] + (4.0 - 4.0 * a) * v + a * nb), spread)

    for x in range(-2, cx + 2):
        value = correction(x)
        for e in (own + 2 * x, own + 2 * x + 1):
            if 0 <= e < nx + 6:
                u3[e] = u2[e] + value
    fix = smooth_strip(l_sides, c_sides, c_strip)
    fix = exact(jnp.concatenate([fix[:, :128], fix[:, 128:]], axis=0), spread_strip)
    third = second + jnp.concatenate([fix[:levels], fix[levels:]], axis=1)
    for e in range(1, nx + 5):
        u4[e] = smooth(u3, third, e)
    fourth = smooth_strip(third, rhs_strip, a_strip)
    for e in range(2, nx + 4):
        p[e] = smooth(u4, fourth, e)
    fifth = smooth_strip(fourth, rhs_strip, a_strip)
    for x in range(nx):
        u, h = horizontal(p, fifth, own + x)
        p_out[:, x, :] = u
        r_out[:, x, :] = h - vertical(u)

    for name in names:
        for copy, goes, _ in copies(name):
            @pl.when(goes)
            def _():
                copy.wait_send()
    for right, left, s in scans:
        @pl.when(w < n_w - s)
        def _():
            right.wait_send()

        @pl.when(w >= s)
        def _():
            left.wait_send()


def local(n_w, n_n, rhs, areas, stiffness):
    levels, nx, ny = rhs.shape
    cx = nx // 2
    steps = max(1, (n_w - 1).bit_length())
    vmem = lambda *shape: pltpu.VMEM(shape, f32)
    whole = pl.BlockSpec(memory_space=pltpu.VMEM)
    return pl.pallas_call(
        functools.partial(kernel, n_w, n_n, nx, ny, levels),
        out_shape=[jax.ShapeDtypeStruct(rhs.shape, f32)] * 2,
        in_specs=[whole, whole, pl.BlockSpec(memory_space=pltpu.SMEM)],
        out_specs=[whole, whole],
        scratch_shapes=[vmem(nx + 6, levels, ny)] * 6
        + [
            vmem(3 * nx, ny), vmem(cx + 8, levels, 128), vmem(cx + 8, levels, 128),
            vmem(5, levels, 128), vmem(6, levels, 128), vmem(2, 2, levels, 128),
            vmem(16, 128), vmem(2, 16, 128),
            vmem(steps, levels, 128), vmem(steps, levels, 128),
            vmem(steps, levels, 128), vmem(steps, levels, 128),
            vmem(levels, 128), vmem(levels, 128), vmem(levels, 128),
            pltpu.SemaphoreType.DMA((9, 2)), pltpu.SemaphoreType.DMA((9, 2)),
            pltpu.SemaphoreType.DMA((steps, 2)), pltpu.SemaphoreType.DMA((steps, 2)),
        ],
        compiler_params=pltpu.CompilerParams(
            collective_id=0, has_side_effects=True, vmem_limit_bytes=40 * 1024 * 1024
        ),
        cost_estimate=pl.CostEstimate(flops=80_000_000, bytes_accessed=1_600_000, transcendentals=0),
    )(rhs, areas, stiffness)


def solution(mesh):
    placed = (P(None, "wide", "narrow"), P("wide", "narrow"), P())
    return jax.shard_map(
        functools.partial(local, mesh.shape["wide"], mesh.shape["narrow"]),
        mesh=mesh,
        in_specs=placed,
        out_specs=(P(None, "wide", "narrow"), P(None, "wide", "narrow")),
        check_vma=False,
    )
```

time: 46.8 us -> 42 us (0.90)
  the two profiles are of different devices: /device:TPU:0 before, /device:TPU:1 now
where the time goes in v2:
time: 42 us; the launch traced here: 41.8 us
  Pallas kernels  37.2 us (89%)
  local copies, waits for them, and re-layouts  3.97 us (9%)
  between operations  0.65 us (2%)
    pallas_call x1, Pallas kernels, local(): pl.pallas_call(functools.partial(kernel, n_w, n_n, nx, ny, levels), out_s...  37.2 us
    unnamed x8, local copies, waits for them, and re-layouts  3.97 us

profile of v2, /device:TPU:1, one launch (start us, length us, event | category | flops | bytes accessed | tf_op | source)
XLA Modules:
  0.0 41.8 jit_solution(8089722457032891832)
XLA Ops:
  0.6 0.0 copy-start
  0.6 1.0 %copy-done = f32[64,8,256]{2,1,0:T(8,128)S(1)} copy-done((f32[64,8,256]{2,1,0:T(8,128)S(1)}, f32[64,8,256]{2,1,0:T(8,128)}, u32[]{:S(2)}) %copy-start) | copy-done | bytes 524312
  1.7 0.0 copy-start.1
  1.7 0.7 %copy-done.1 = f32[8,256]{1,0:T(8,128)S(1)} copy-done((f32[8,256]{1,0:T(8,128)S(1)}, f32[8,256]{1,0:T(8,128)}, u32[]{:S(2)}) %copy-start.1) | copy-done | bytes 8216
  2.4 0.0 copy-start.2
  2.4 0.7 %copy-done.2 = f32[64]{0:T(128)S(1)} copy-done((f32[64]{0:T(128)S(1)}, f32[64]{0:T(128)}, u32[]{:S(2)}) %copy-start.2) | copy-done | bytes 280
  3.0 37.2 %shard_map.50 = (f32[64,8,256]{2,1,0:T(8,128)S(1)}, f32[64,8,256]{2,1,0:T(8,128)S(1)}) custom-call(f32[64,8,256]{2,1,0:T(8,128)S(1)} %copy-done, f32[8,256]{1,0:T(8,128)S(1)} %copy-done.1, f32[64]{0:T(128)S(1)} %copy-done.2), custom_call_target="tpu_custom_call" | custom-call | flops 80000000 | bytes 1600000 | tf_op jit(solution)/shard_map/pallas_call | solution.py:467
  40.2 0.8 %copy.7 = f32[64,8,256]{2,1,0:T(8,128)} copy(f32[64,8,256]{2,1,0:T(8,128)S(1)} %get-tuple-element.4) | data formatting | bytes 1048576
  41.0 0.8 %copy.8 = f32[64,8,256]{2,1,0:T(8,128)} copy(f32[64,8,256]{2,1,0:T(8,128)S(1)} %get-tuple-element.5) | data formatting | bytes 1048576
Async XLA Ops:
  0.6 1.0 %copy-start = (f32[64,8,256]{2,1,0:T(8,128)S(1)}, f32[64,8,256]{2,1,0:T(8,128)}, u32[]{:S(2)}) copy-start(f32[64,8,256]{2,1,0:T(8,128)} %rhs_ref.1) | copy-start | bytes 1572868
  1.7 0.7 %copy-start.1 = (f32[8,256]{1,0:T(8,128)S(1)}, f32[8,256]{1,0:T(8,128)}, u32[]{:S(2)}) copy-start(f32[8,256]{1,0:T(8,128)} %areas_ref.1) | copy-start | bytes 24580
  2.4 0.7 %copy-start.2 = (f32[64]{0:T(128)S(1)}, f32[64]{0:T(128)}, u32[]{:S(2)}) copy-start(f32[64]{0:T(128)} %stiff_ref.1) | copy-start | bytes 772

commit v3 on v2

--- a/solution.py
+++ b/solution.py
@@ -20,7 +20,7 @@
 def kernel(
     n_w, n_n, nx, ny, levels,
     rhs_ref, areas_ref, stiff_ref, p_out, r_out,
-    rhs_x, u1, u2, u3, u4, p, wide_a, coarse, line, pack, strip, corner, pack_a, strip_a,
+    rhs_x, u1, u2, u3, u4, p, wide_a, coarse, line, pack, strip, corner, pack_a, strip_a, coef_at,
     scan_f, scan_z, scan_rf, scan_rz, theta, phi, stiff_b,
     send_sem, recv_sem, scan_send, scan_recv,
 ):
@@ -37,6 +37,7 @@
     while (1 << len(strides)) < n_w:
         strides.append(1 << len(strides))
     own = 3
+    tiles = ny // 128
 
     small = jnp.zeros((levels, 128), f32)
     nothing = jnp.zeros((levels, ny), f32)
@@ -44,15 +45,13 @@
         ((1, 2), (0, 1), (0, 1, 2, 3)),
         ((nx + 3, nx + 4), (nx + 4, nx + 5), (cx + 4, cx + 5, cx + 6, cx + 7)),
     )
-    rhs_x[0] = nothing
-    rhs_x[nx + 5] = nothing
     for side in range(2):
         @pl.when(jnp.logical_not(has[side]))
         def _():
             for e in edge_x[side][0]:
-                rhs_x[e] = nothing
+                rhs_x[e + 1] = nothing
             for e in edge_x[side][1]:
-                u2[e] = nothing
+                u2[e + 1] = nothing
             for e in edge_x[side][2]:
                 coarse[e] = small
             corner[0, side] = small
@@ -95,11 +94,11 @@
     exchanges = {
         "areas": (0, (wide_a.at[pl.ds(nx, nx)], wide_a.at[pl.ds(2 * nx, nx)]),
                   (wide_a.at[pl.ds(nx, nx)], wide_a.at[pl.ds(0, nx)])),
-        "rhs": (0, (rhs_x.at[pl.ds(own, 2)], rhs_x.at[pl.ds(own + nx, 2)]),
-                (rhs_x.at[pl.ds(own + nx - 2, 2)], rhs_x.at[pl.ds(own - 2, 2)])),
+        "rhs": (0, (rhs_x.at[pl.ds(own + 1, 2)], rhs_x.at[pl.ds(own + nx + 1, 2)]),
+                (rhs_x.at[pl.ds(own + nx - 2 + 1, 2)], rhs_x.at[pl.ds(own - 2 + 1, 2)])),
         "corner": (0, (pack.at[1], corner.at[0, 1]), (pack.at[1], corner.at[0, 0])),
-        "u2": (0, (u2.at[pl.ds(own + 1, 2)], u2.at[pl.ds(own + nx + 1, 2)]),
-               (u2.at[pl.ds(own + nx - 3, 2)], u2.at[pl.ds(own - 3, 2)])),
+        "u2": (0, (u2.at[pl.ds(own + 1 + 1, 2)], u2.at[pl.ds(own + nx + 1 + 1, 2)]),
+               (u2.at[pl.ds(own + nx - 3 + 1, 2)], u2.at[pl.ds(own - 3 + 1, 2)])),
         "u2corner": (0, (pack.at[2], corner.at[1, 1]), (pack.at[2], corner.at[1, 0])),
         "coarse": (0, (coarse.at[pl.ds(4, cx)], coarse.at[pl.ds(4 + cx, cx)]),
                    (coarse.at[pl.ds(4, cx)], coarse.at[pl.ds(4 - cx, cx)])),
@@ -143,39 +142,55 @@
     inner = lane_c % 8 < 4
     row_c = lane_c // 8
 
-    def packed(rows, base=None):
-        result = jnp.zeros((levels, 128), f32) if base is None else base
-        for e, value in rows:
+    def packed(get, start_at, stop_at, base=None):
+        def body(e, result):
+            value = get(e)
             ends = jnp.where(lane_c < 4, value[:, :128], value[:, value.shape[1] - 128 :])
-            result = jnp.where(row_c == e, pltpu.roll(ends, 8 * e + 4, 1), result)
-        return result
+            return jnp.where(row_c == e, pltpu.roll(ends, 8 * e + 4, 1), result)
+
+        return lax.fori_loop(start_at, stop_at, body, jnp.zeros((levels, 128), f32) if base is None else base, unroll=2)
+
+    def pairs(count, body):
+        def both(i, carry):
+            body(2 * i)
+            body(2 * i + 1)
+            return carry
+
+        lax.fori_loop(0, count // 2, both, 0)
 
     def strips(mine, low, high):
         return jnp.concatenate([jnp.where(inner, low, mine), jnp.where(inner, mine, high)], axis=1)
 
     wide_a[nx : 2 * nx, :] = areas_ref[...]
     for x in (0, 1, nx - 2, nx - 1) + tuple(range(2, nx - 2)):
-        rhs_x[own + x] = rhs_ref[:, x, :]
+        rhs_x[own + x + 1] = jnp.concatenate(
+            [rhs_ref[pl.ds(x + nx * t, levels, stride=tiles * nx), :] for t in range(tiles)], axis=1
+        )
     peers = sum(h.astype(jnp.int32) for h in has)
     for s in strides[1:]:
         peers = peers + (w >= s).astype(jnp.int32) + (w < n_w - s).astype(jnp.int32)
     pl.semaphore_wait(barrier, peers)
     start("areas")
     start("rhs")
-    pack_rhs = packed([(e, rhs_x[e]) for e in range(own, own + nx)])
+    pack_rhs = packed(lambda e: rhs_x[e + 1], own, own + nx)
     pack[0] = pack_rhs
     start("strip")
 
-    before, now = jnp.float32(0.0), jnp.float32(1.0)
-    for i in range(levels):
-        theta[i : i + 1, :] = jnp.full((1, 128), now, f32)
-        before, now = now, (stiff_ref[i] * 0.125 + 1.0) * now - 0.0625 * before
-        stiff_b[i : i + 1, :] = jnp.full((1, 128), stiff_ref[i], f32)
+    def minors(i, carry):
+        t_before, t_now, p_before, p_now = carry
+        j = levels - 1 - i
+        here, there = stiff_ref[i], stiff_ref[j]
+        theta[pl.ds(i, 1), :] = jnp.full((1, 128), t_now, f32)
+        phi[pl.ds(j, 1), :] = jnp.full((1, 128), p_now, f32)
+        stiff_b[pl.ds(i, 1), :] = jnp.full((1, 128), here, f32)
+        return (
+            t_now, (here * 0.125 + 1.0) * t_now - 0.0625 * t_before,
+            p_now, (there * 0.125 + 1.0) * p_now - 0.0625 * p_before,
+        )
+
+    zero, one = jnp.float32(0.0), jnp.float32(1.0)
+    now = lax.fori_loop(0, levels, minors, (zero, one, zero, one), unroll=8)[1]
     whole = jnp.full((levels, 128), now, f32)
-    before, now = jnp.float32(0.0), jnp.float32(1.0)
-    for i in reversed(range(levels)):
-        phi[i : i + 1, :] = jnp.full((1, 128), now, f32)
-        before, now = now, (stiff_ref[i] * 0.125 + 1.0) * now - 0.0625 * before
     row = lax.broadcasted_iota(jnp.int32, (levels, 128), 0)
     col = lax.broadcasted_iota(jnp.int32, (levels, 128), 1)
     apart = jnp.abs(row - col)
@@ -196,7 +211,7 @@
         return jnp.dot(weights, stacked, preferred_element_type=f32)
 
     def area(e):
-        return wide_a[nx + e - own : nx + e - own + 1, :]
+        return wide_a[pl.ds(nx + e - own, 1), :]
 
     def sides(u, sides_of, e):
         n = u.shape[1]
@@ -211,19 +226,19 @@
         return down + jnp.where(index == n - 1, edge, pltpu.roll(u, n - 1, 1))
 
     def smooth(field, sides_of, e):
-        u = field[e]
-        nb = field[e - 1] + field[e + 1] + sides(u, sides_of, e)
+        u = field[e + 1]
+        nb = field[e] + field[e + 2] + sides(u, sides_of, e)
         a = area(e)
-        return 0.6 * u + apply(rhs_x[e] + (4.0 - 4.0 * a) * u + a * nb)
+        return 0.6 * u + apply(rhs_x[e + 1] + (4.0 - 4.0 * a) * u + a * nb)
 
     def smooth_strip(s, right_side, a):
         nb = pltpu.roll(s, 1, 1) + pltpu.roll(s, ny - 1, 1) + pltpu.roll(s, 8, 1) + pltpu.roll(s, ny - 8, 1)
         return 0.6 * s + apply(right_side + (4.0 - 4.0 * a) * s + a * nb)
 
     def horizontal(field, sides_of, e):
-        u = field[e]
-        nb = field[e - 1] + field[e + 1] + sides(u, sides_of, e)
-        return u, rhs_x[e] - area(e) * (4.0 * u - nb)
+        u = field[e + 1]
+        nb = field[e] + field[e + 2] + sides(u, sides_of, e)
+        return u, rhs_x[e + 1] - area(e) * (4.0 * u - nb)
 
     def vertical(v):
         above = jnp.where(level == levels - 1, 0.0, pltpu.roll(v, levels - 1, 0))
@@ -252,29 +267,40 @@
         both = jnp.dot(jnp.concatenate([high, low], axis=0), matrix, preferred_element_type=f32)
         return both[:rows] + both[rows:]
 
-    for e in range(own, own + nx):
-        u1[e] = apply(rhs_x[e])
+    def first_own(i):
+        u1[own + i + 1] = apply(rhs_x[own + i + 1])
+
+    pairs(nx, first_own)
 
     arrive("strip")
     halo = jnp.where(inner, strip[0], strip[1])
     pack[1] = halo
     start("corner")
     first = apply(strips(pack_rhs, halo, halo))
-    for e in range(own + 1, own + nx - 1):
-        u2[e] = smooth(u1, first, e)
+    first_own_strip = first
+
+    def second_own(i):
+        e = own + 1 + i
+        u2[e + 1] = smooth(u1, first_own_strip, e)
+
+    pairs(nx - 2, second_own)
 
     arrive("areas")
     eight = lane_c[:8]
-    packed_a = jnp.zeros((8, 128), f32)
-    for e in range(0, nx + 6):
+
+    def put_area(e, result):
         v = jnp.broadcast_to(area(e), (8, ny))
         v = pltpu.roll(jnp.where(eight < 4, v[:, :128], v[:, ny - 128 :]), 8 * e + 4, 1)
-        packed_a = jnp.where(eight // 8 == e, v, packed_a)
+        return jnp.where(eight // 8 == e, v, result)
+
+    packed_a = lax.fori_loop(0, nx + 6, put_area, jnp.zeros((8, 128), f32), unroll=2)
     sums = []
     for x in range(-2, cx + 2):
         at = nx + 2 * x
         sums.append(jnp.broadcast_to(0.0625 * (wide_a[at : at + 1, :] + wide_a[at + 1 : at + 2, :]), (8, ny)))
     coef = exact(jnp.concatenate(sums, axis=0), pick)
+    for x in range(cx + 4):
+        coef_at[x] = coef[8 * x : 8 * x + 8]
     coef = {x: coef[8 * (x + 2) : 8 * (x + 2) + 8] for x in range(-2, cx + 2)}
     packed_c = jnp.zeros((8, 128), f32)
     for x in range(-2, cx + 2):
@@ -285,10 +311,13 @@
     start("strip_a")
 
     arrive("rhs")
-    outer = (own - 2, own - 1, own + nx, own + nx + 1)
-    for e in outer:
-        u1[e] = apply(rhs_x[e])
-    pack_all = packed([(e, rhs_x[e]) for e in outer], pack_rhs)
+    def first_outer(i):
+        e = own - 2 + i % 2 + (nx + 2) * (i // 2)
+        u1[e + 1] = apply(rhs_x[e + 1])
+
+    pairs(4, first_outer)
+    pack_all = packed(lambda e: rhs_x[e + 1], own - 2, own, pack_rhs)
+    pack_all = packed(lambda e: rhs_x[e + 1], own + nx, own + nx + 2, pack_all)
     arrive("corner", "strip_a")
     halo = jnp.where(
         row_c < own, pltpu.roll(corner[0, 0], 64, 1),
@@ -303,8 +332,12 @@
     a_strip = strips_a(strip_a[0, 0:8, :], strip_a[1, 0:8, :], packed_a)
     c_strip = strips_a(strip_a[0, 8:16, :], strip_a[1, 8:16, :], packed_c)
     first = apply(rhs_strip)
-    for e in (own - 1, own, own + nx - 1, own + nx):
-        u2[e] = smooth(u1, first, e)
+
+    def second_outer(i):
+        e = own - 1 + i % 2 + nx * (i // 2)
+        u2[e + 1] = smooth(u1, first, e)
+
+    pairs(4, second_outer)
     second = smooth_strip(first, rhs_strip, a_strip)
 
     s = stiff_b[...]
@@ -323,11 +356,13 @@
     tail = jnp.where(is_last, power[0], far * power[2 * cx])
     scale = keep / (1.0 + r)
 
-    for x in range(cx):
+    def to_coarse(x):
         e = own + 2 * x
         u_a, h_a = horizontal(u2, second, e)
         u_b, h_b = horizontal(u2, second, e + 1)
         coarse[4 + x] = exact(0.25 * (h_a + h_b - vertical(u_a + u_b)), pick)
+
+    pairs(cx, to_coarse)
     mine = [coarse[4 + x] for x in range(cx)]
     forward = mine[0]
     for x in range(1, cx):
@@ -401,8 +436,8 @@
         if t >= cx:
             value = jnp.where(is_last, 0.0, value)
         line[4 + t] = value
-    pack_c = packed([(t + 3, coarse[4 + t]) for t in range(-3, cx + 3)])
-    pack_l = packed([(t + 3, line[4 + t]) for t in range(-3, cx + 3)])
+    pack_c = packed(lambda e: coarse[e + 1], 0, cx + 6)
+    pack_l = packed(lambda e: line[e + 1], 0, cx + 6)
     pack[3] = pack_c
     pack[4] = pack_l
     start("line")
@@ -412,7 +447,7 @@
         row_c < own - 1, pltpu.roll(corner[1, 0], 64, 1),
         jnp.where(row_c > own + nx, pltpu.roll(corner[1, 1], 64, 1), pack[2]),
     )
-    second = strips(packed([(e, u2[e]) for e in range(nx + 6)]), halo, halo)
+    second = strips(packed(lambda e: u2[e + 1], 0, nx + 6), halo, halo)
 
     arrive("line")
     c_sides = strips(pack_c, strip[2], strip[4])
@@ -421,27 +456,40 @@
     def correction(x):
         v = line[4 + x]
         nb = line[3 + x] + line[5 + x] + sides(v, l_sides, x + 3)
-        a = coef[x][:1]
+        a = coef_at[x + 2][:1]
         return exact(0.6 * v + apply(coarse[4 + x] + (4.0 - 4.0 * a) * v + a * nb), spread)
 
-    for x in range(-2, cx + 2):
-        value = correction(x)
-        for e in (own + 2 * x, own + 2 * x + 1):
-            if 0 <= e < nx + 6:
-                u3[e] = u2[e] + value
+    def third_rows(i):
+        value = correction(i - 2)
+        for e in (own + 2 * i - 4, own + 2 * i - 3):
+            u3[e + 1] = u2[e + 1] + value
+
+    pairs(cx + 4, third_rows)
     fix = smooth_strip(l_sides, c_sides, c_strip)
     fix = exact(jnp.concatenate([fix[:, :128], fix[:, 128:]], axis=0), spread_strip)
     third = second + jnp.concatenate([fix[:levels], fix[levels:]], axis=1)
-    for e in range(1, nx + 5):
-        u4[e] = smooth(u3, third, e)
+
+    def fourth_rows(i):
+        u4[i + 2] = smooth(u3, third, i + 1)
+
+    pairs(nx + 4, fourth_rows)
     fourth = smooth_strip(third, rhs_strip, a_strip)
-    for e in range(2, nx + 4):
-        p[e] = smooth(u4, fourth, e)
+
+    def fifth_rows(i):
+        p[i + 3] = smooth(u4, fourth, i + 2)
+
+    pairs(nx + 2, fifth_rows)
     fifth = smooth_strip(fourth, rhs_strip, a_strip)
-    for x in range(nx):
+
+    def last_rows(x):
         u, h = horizontal(p, fifth, own + x)
-        p_out[:, x, :] = u
-        r_out[:, x, :] = h - vertical(u)
+        left_over = h - vertical(u)
+        for t in range(tiles):
+            at = pl.ds(x + nx * t, levels, stride=tiles * nx)
+            p_out[at, :] = u[:, 128 * t : 128 * t + 128]
+            r_out[at, :] = left_over[:, 128 * t : 128 * t + 128]
+
+    pairs(nx, last_rows)
 
     for name in names:
         for copy, goes, _ in copies(name):
@@ -460,20 +508,20 @@
 
 def local(n_w, n_n, rhs, areas, stiffness):
     levels, nx, ny = rhs.shape
-    cx = nx // 2
+    cx, tiles = nx // 2, ny // 128
     steps = max(1, (n_w - 1).bit_length())
     vmem = lambda *shape: pltpu.VMEM(shape, f32)
     whole = pl.BlockSpec(memory_space=pltpu.VMEM)
-    return pl.pallas_call(
+    outs = pl.pallas_call(
         functools.partial(kernel, n_w, n_n, nx, ny, levels),
-        out_shape=[jax.ShapeDtypeStruct(rhs.shape, f32)] * 2,
+        out_shape=[jax.ShapeDtypeStruct((levels * nx * tiles, 128), f32)] * 2,
         in_specs=[whole, whole, pl.BlockSpec(memory_space=pltpu.SMEM)],
         out_specs=[whole, whole],
-        scratch_shapes=[vmem(nx + 6, levels, ny)] * 6
+        scratch_shapes=[vmem(nx + 8, levels, ny)] * 6
         + [
             vmem(3 * nx, ny), vmem(cx + 8, levels, 128), vmem(cx + 8, levels, 128),
             vmem(5, levels, 128), vmem(6, levels, 128), vmem(2, 2, levels, 128),
-            vmem(16, 128), vmem(2, 16, 128),
+            vmem(16, 128), vmem(2, 16, 128), vmem(cx + 4, 8, 128),
             vmem(steps, levels, 128), vmem(steps, levels, 128),
             vmem(steps, levels, 128), vmem(steps, levels, 128),
             vmem(levels, 128), vmem(levels, 128), vmem(levels, 128),
@@ -484,7 +532,8 @@
             collective_id=0, has_side_effects=True, vmem_limit_bytes=40 * 1024 * 1024
         ),
         cost_estimate=pl.CostEstimate(flops=80_000_000, bytes_accessed=1_600_000, transcendentals=0),
-    )(rhs, areas, stiffness)
+    )(rhs.reshape(levels, nx, tiles, 128).transpose(0, 2, 1, 3).reshape(-1, 128), areas, stiffness)
+    return tuple(v.reshape(levels, tiles, nx, 128).transpose(0, 2, 1, 3).reshape(rhs.shape) for v in outs)
 
 
 def solution(mesh):

time: 42 us -> 48.2 us (1.15)
  Pallas kernels: 37.2 us -> 43.4 us
    pallas_call x1, Pallas kernels: 37.2 us -> 43.4 us  [local(): pl.pallas_call(functools.partial(kernel, n_w, n_n, nx, ny, levels), out_s...]
where the time goes in v3:
time: 48.2 us; the launch traced here: 48 us
  Pallas kernels  43.4 us (90%)
  local copies, waits for them, and re-layouts  3.97 us (8%)
  between operations  0.65 us (1%)
    pallas_call x1, Pallas kernels, local(): pl.pallas_call(functools.partial(kernel, n_w, n_n, nx, ny, levels), out_s...  43.4 us
    unnamed x8, local copies, waits for them, and re-layouts  3.97 us

profile of v3, /device:TPU:1, one launch (start us, length us, event | category | flops | bytes accessed | tf_op | source)
XLA Modules:
  0.0 48.0 jit_solution(2119880455806791877)
XLA Ops:
  0.6 0.0 copy-start.2
  0.6 0.6 %copy-done.2 = f32[64]{0:T(128)S(1)} copy-done((f32[64]{0:T(128)S(1)}, f32[64]{0:T(128)}, u32[]{:S(2)}) %copy-start.2) | copy-done | bytes 280
  1.3 0.0 copy-start
  1.3 1.0 %copy-done = f32[64,8,256]{2,1,0:T(8,128)S(1)} copy-done((f32[64,8,256]{2,1,0:T(8,128)S(1)}, f32[64,8,256]{2,1,0:T(8,128)}, u32[]{:S(2)}) %copy-start) | copy-done | bytes 524312
  2.3 0.0 copy-start.1
  2.3 0.7 %copy-done.1 = f32[8,256]{1,0:T(8,128)S(1)} copy-done((f32[8,256]{1,0:T(8,128)S(1)}, f32[8,256]{1,0:T(8,128)}, u32[]{:S(2)}) %copy-start.1) | copy-done | bytes 8216
  3.0 43.4 %shard_map.50 = (f32[1024,128]{1,0:T(8,128)S(1)}, f32[1024,128]{1,0:T(8,128)S(1)}) custom-call(f32[1024,128]{1,0:T(8,128)S(1)} %bitcast.15, f32[8,256]{1,0:T(8,128)S(1)} %copy-done.1, f32[64]{0:T(128)S(1)} %copy-done.2), custom_call_target="tpu_custom_call" | custom-call | flops 80000000 | bytes 1600000 | tf_op jit(solution)/shard_map/pallas_call | solution.py:515
  46.4 0.8 %copy.7 = f32[64,8,256]{2,1,0:T(8,128)} copy(f32[64,8,256]{2,1,0:T(8,128)S(1)} %bitcast.17) | data formatting | bytes 1048576
  47.2 0.8 %copy.8 = f32[64,8,256]{2,1,0:T(8,128)} copy(f32[64,8,256]{2,1,0:T(8,128)S(1)} %bitcast.16) | data formatting | bytes 1048576
Async XLA Ops:
  0.6 0.7 %copy-start.2 = (f32[64]{0:T(128)S(1)}, f32[64]{0:T(128)}, u32[]{:S(2)}) copy-start(f32[64]{0:T(128)} %stiff_ref.1) | copy-start | bytes 772
  1.3 1.0 %copy-start = (f32[64,8,256]{2,1,0:T(8,128)S(1)}, f32[64,8,256]{2,1,0:T(8,128)}, u32[]{:S(2)}) copy-start(f32[64,8,256]{2,1,0:T(8,128)} %param.3) | copy-start | bytes 1572868
  2.3 0.7 %copy-start.1 = (f32[8,256]{1,0:T(8,128)S(1)}, f32[8,256]{1,0:T(8,128)}, u32[]{:S(2)}) copy-start(f32[8,256]{1,0:T(8,128)} %areas_ref.1) | copy-start | bytes 24580

commit v4 on v2

--- a/solution.py
+++ b/solution.py
@@ -20,7 +20,7 @@
 def kernel(
     n_w, n_n, nx, ny, levels,
     rhs_ref, areas_ref, stiff_ref, p_out, r_out,
-    rhs_x, u1, u2, u3, u4, p, wide_a, coarse, line, pack, strip, corner, pack_a, strip_a,
+    rhs_x, u1, u2, u3, u4, p, wide_a, coarse, line, pack, strip, corner_of, corner, pack_a, strip_a,
     scan_f, scan_z, scan_rf, scan_rz, theta, phi, stiff_b,
     send_sem, recv_sem, scan_send, scan_recv,
 ):
@@ -37,12 +37,13 @@
     while (1 << len(strides)) < n_w:
         strides.append(1 << len(strides))
     own = 3
+    tiles = ny // 128
 
     small = jnp.zeros((levels, 128), f32)
     nothing = jnp.zeros((levels, ny), f32)
     edge_x = (
-        ((1, 2), (0, 1), (0, 1, 2, 3)),
-        ((nx + 3, nx + 4), (nx + 4, nx + 5), (cx + 4, cx + 5, cx + 6, cx + 7)),
+        ((1, 2), (0, 1), (2, 3)),
+        ((nx + 3, nx + 4), (nx + 4, nx + 5), (cx + 4, cx + 5)),
     )
     rhs_x[0] = nothing
     rhs_x[nx + 5] = nothing
@@ -55,8 +56,8 @@
                 u2[e] = nothing
             for e in edge_x[side][2]:
                 coarse[e] = small
-            corner[0, side] = small
-            corner[1, side] = small
+            corner[0, side] = small[:8]
+            corner[1, side] = small[:8]
             wide_a[2 * side * nx : 2 * side * nx + nx, :] = jnp.zeros((nx, ny), f32)
 
         @pl.when(jnp.logical_not(has[2 + side]))
@@ -97,15 +98,15 @@
                   (wide_a.at[pl.ds(nx, nx)], wide_a.at[pl.ds(0, nx)])),
         "rhs": (0, (rhs_x.at[pl.ds(own, 2)], rhs_x.at[pl.ds(own + nx, 2)]),
                 (rhs_x.at[pl.ds(own + nx - 2, 2)], rhs_x.at[pl.ds(own - 2, 2)])),
-        "corner": (0, (pack.at[1], corner.at[0, 1]), (pack.at[1], corner.at[0, 0])),
-        "u2": (0, (u2.at[pl.ds(own + 1, 2)], u2.at[pl.ds(own + nx + 1, 2)]),
-               (u2.at[pl.ds(own + nx - 3, 2)], u2.at[pl.ds(own - 3, 2)])),
-        "u2corner": (0, (pack.at[2], corner.at[1, 1]), (pack.at[2], corner.at[1, 0])),
-        "coarse": (0, (coarse.at[pl.ds(4, cx)], coarse.at[pl.ds(4 + cx, cx)]),
-                   (coarse.at[pl.ds(4, cx)], coarse.at[pl.ds(4 - cx, cx)])),
+        "corner": (0, (corner_of.at[0, 0], corner.at[0, 1]), (corner_of.at[0, 1], corner.at[0, 0])),
+        "u2near": (0, (u2.at[own + 1], u2.at[own + nx + 1]), (u2.at[own + nx - 2], u2.at[own - 2])),
+        "u2far": (0, (u2.at[own + 2], u2.at[own + nx + 2]), (u2.at[own + nx - 3], u2.at[own - 3])),
+        "u2corner": (0, (corner_of.at[1, 0], corner.at[1, 1]), (corner_of.at[1, 1], corner.at[1, 0])),
+        "coarse": (0, (coarse.at[pl.ds(4, 2)], coarse.at[pl.ds(4 + cx, 2)]),
+                   (coarse.at[pl.ds(2 + cx, 2)], coarse.at[pl.ds(2, 2)])),
         "strip": (1, (pack.at[0], strip.at[1]), (pack.at[0], strip.at[0])),
         "strip_a": (1, (pack_a, strip_a.at[1]), (pack_a, strip_a.at[0])),
-        "line": (1, (pack.at[pl.ds(3, 2)], strip.at[pl.ds(4, 2)]), (pack.at[pl.ds(3, 2)], strip.at[pl.ds(2, 2)])),
+        "line": (1, (pack.at[pl.ds(1, 2)], strip.at[pl.ds(4, 2)]), (pack.at[pl.ds(1, 2)], strip.at[pl.ds(2, 2)])),
     }
     names = list(exchanges)
 
@@ -153,9 +154,21 @@
     def strips(mine, low, high):
         return jnp.concatenate([jnp.where(inner, low, mine), jnp.where(inner, mine, high)], axis=1)
 
+    def squeeze(tile, e):
+        result = jnp.zeros((8, 128), f32)
+        for b in range(levels // 8):
+            part = pltpu.roll(tile[8 * b : 8 * b + 8], (16 * b - 8 * e) % 128, 1)
+            result = jnp.where(lane_c[:8] // 16 == b, part, result)
+        return result
+
+    def unsqueeze(tile, e):
+        return jnp.concatenate([pltpu.roll(tile, (8 * e - 16 * b) % 128, 1) for b in range(levels // 8)], axis=0)
+
     wide_a[nx : 2 * nx, :] = areas_ref[...]
     for x in (0, 1, nx - 2, nx - 1) + tuple(range(2, nx - 2)):
-        rhs_x[own + x] = rhs_ref[:, x, :]
+        rhs_x[own + x] = jnp.concatenate(
+            [rhs_ref[pl.ds(x + nx * t, levels, stride=tiles * nx), :] for t in range(tiles)], axis=1
+        )
     peers = sum(h.astype(jnp.int32) for h in has)
     for s in strides[1:]:
         peers = peers + (w >= s).astype(jnp.int32) + (w < n_w - s).astype(jnp.int32)
@@ -166,16 +179,17 @@
     pack[0] = pack_rhs
     start("strip")
 
-    before, now = jnp.float32(0.0), jnp.float32(1.0)
+    zero, one = jnp.float32(0.0), jnp.float32(1.0)
+    t_before, t_now, p_before, p_now = zero, one, zero, one
     for i in range(levels):
-        theta[i : i + 1, :] = jnp.full((1, 128), now, f32)
-        before, now = now, (stiff_ref[i] * 0.125 + 1.0) * now - 0.0625 * before
-        stiff_b[i : i + 1, :] = jnp.full((1, 128), stiff_ref[i], f32)
-    whole = jnp.full((levels, 128), now, f32)
-    before, now = jnp.float32(0.0), jnp.float32(1.0)
-    for i in reversed(range(levels)):
-        phi[i : i + 1, :] = jnp.full((1, 128), now, f32)
-        before, now = now, (stiff_ref[i] * 0.125 + 1.0) * now - 0.0625 * before
+        j = levels - 1 - i
+        here, there = stiff_ref[i], stiff_ref[j]
+        theta[i : i + 1, :] = jnp.full((1, 128), t_now, f32)
+        phi[j : j + 1, :] = jnp.full((1, 128), p_now, f32)
+        stiff_b[i : i + 1, :] = jnp.full((1, 128), here, f32)
+        t_before, t_now = t_now, (here * 0.125 + 1.0) * t_now - 0.0625 * t_before
+        p_before, p_now = p_now, (there * 0.125 + 1.0) * p_now - 0.0625 * p_before
+    whole = jnp.full((levels, 128), t_now, f32)
     row = lax.broadcasted_iota(jnp.int32, (levels, 128), 0)
     col = lax.broadcasted_iota(jnp.int32, (levels, 128), 1)
     apart = jnp.abs(row - col)
@@ -257,7 +271,8 @@
 
     arrive("strip")
     halo = jnp.where(inner, strip[0], strip[1])
-    pack[1] = halo
+    corner_of[0, 0] = squeeze(halo, own)
+    corner_of[0, 1] = squeeze(halo, own + nx - 2)
     start("corner")
     first = apply(strips(pack_rhs, halo, halo))
     for e in range(own + 1, own + nx - 1):
@@ -285,14 +300,15 @@
     start("strip_a")
 
     arrive("rhs")
+    start("u2near")
     outer = (own - 2, own - 1, own + nx, own + nx + 1)
     for e in outer:
         u1[e] = apply(rhs_x[e])
     pack_all = packed([(e, rhs_x[e]) for e in outer], pack_rhs)
     arrive("corner", "strip_a")
     halo = jnp.where(
-        row_c < own, pltpu.roll(corner[0, 0], 64, 1),
-        jnp.where(row_c >= own + nx, pltpu.roll(corner[0, 1], 64, 1), halo),
+        row_c < own, unsqueeze(corner[0, 0], own - 2),
+        jnp.where(row_c >= own + nx, unsqueeze(corner[0, 1], own + nx), halo),
     )
     rhs_strip = strips(pack_all, halo, halo)
     inner_a = eight % 8 < 4
@@ -311,7 +327,7 @@
     keep = jnp.sqrt(s + 0.25 * s * s) - 0.5 * s
     r = 1.0 - keep
     power = [jnp.ones_like(r)]
-    for _ in range(4 * cx):
+    for _ in range(4 * cx + 6):
         power.append(power[-1] * r)
     is_last = w == n_w - 1
     far = jnp.ones_like(r)
@@ -361,8 +377,10 @@
 
         if i == 0:
             start("coarse")
-            start("u2")
-            pack[2] = jnp.where(inner, second[:, :128], second[:, 128:])
+            start("u2far")
+            halo = jnp.where(inner, second[:, :128], second[:, 128:])
+            corner_of[1, 0] = squeeze(halo, own + 1)
+            corner_of[1, 1] = squeeze(halo, own + nx - 3)
             start("u2corner")
 
         @pl.when(w >= s)
@@ -376,41 +394,47 @@
         got_f, got_z = scan_rf[i], scan_rz[i]
         forward = forward + step_all * got_f
         backward = backward + step_all * got_z
-        if i:
-            enter = enter + (got_f if i == 1 else step_less * got_f)
-            leave = leave + (got_z if i == 1 else step_less * got_z)
-            step_less = step_all if i == 1 else step_less * step_all
+        enter = enter + (step_less * got_f if i else got_f)
+        leave = leave + (step_less * got_z if i else got_z)
+        step_less = step_less * step_all if i else step_all
         step_all = step_all * step_all
 
     arrive("coarse")
-    window = range(-4, cx + 4)
-    causal = {-5: enter}
-    beyond = {cx + 3: r * leave}
-    total = enter * jnp.where(is_last, power[2 * cx + 2], far * power[2 * cx + 6])
-    for t in window:
-        value = coarse[4 + t]
-        causal[t] = value + r * causal[t - 1]
-        total = total + value * jnp.where(is_last, power[max(cx + 1 - t, 0)], far * power[2 * cx + 1 - t])
-    for t in reversed(range(-4, cx + 3)):
-        beyond[t] = r * (beyond[t + 1] + coarse[4 + t + 1])
+    inverse_r = 1.0 / r
+    image = {
+        t: 1.0 - jnp.where(is_last, power[max(2 * cx - 2 * t, 0)], far * power[4 * cx - 2 * t])
+        for t in range(-3, cx + 3)
+    }
+    before = {-1: enter}
+    for t in range(cx + 2):
+        before[t] = coarse[4 + t] + r * before[t - 1]
+    for t in (-2, -3):
+        before[t] = (before[t + 1] - coarse[4 + t + 1]) * inverse_r
+    after = {cx: leave}
+    for t in reversed(range(-2, cx)):
+        after[t] = image[t] * coarse[4 + t] + r * after[t + 1]
+    for t in (cx + 1, cx + 2):
+        after[t] = (after[t - 1] - image[t - 1] * coarse[4 + t - 1]) * inverse_r
     for t in range(-3, cx + 3):
-        back = jnp.where(is_last, power[max(cx - 1 - t, 0)], power[cx + 3 - t])
-        value = scale * (causal[t] + beyond[t] - back * total)
+        if t < cx:
+            value = scale * (image[t] * before[t] + r * after[t + 1])
+        else:
+            value = scale * (image[t] * r * before[t - 1] + after[t])
         if t < 0:
             value = jnp.where(w == 0, 0.0, value)
         if t >= cx:
             value = jnp.where(is_last, 0.0, value)
         line[4 + t] = value
-    pack_c = packed([(t + 3, coarse[4 + t]) for t in range(-3, cx + 3)])
+    pack_c = packed([(t + 3, coarse[4 + t]) for t in range(-2, cx + 2)])
     pack_l = packed([(t + 3, line[4 + t]) for t in range(-3, cx + 3)])
-    pack[3] = pack_c
-    pack[4] = pack_l
+    pack[1] = pack_c
+    pack[2] = pack_l
     start("line")
 
-    arrive("u2", "u2corner")
+    arrive("u2near", "u2far", "u2corner")
     halo = jnp.where(
-        row_c < own - 1, pltpu.roll(corner[1, 0], 64, 1),
-        jnp.where(row_c > own + nx, pltpu.roll(corner[1, 1], 64, 1), pack[2]),
+        row_c < own - 1, unsqueeze(corner[1, 0], own - 3),
+        jnp.where(row_c > own + nx, unsqueeze(corner[1, 1], own + nx + 1), halo),
     )
     second = strips(packed([(e, u2[e]) for e in range(nx + 6)]), halo, halo)
 
@@ -440,8 +464,11 @@
     fifth = smooth_strip(fourth, rhs_strip, a_strip)
     for x in range(nx):
         u, h = horizontal(p, fifth, own + x)
-        p_out[:, x, :] = u
-        r_out[:, x, :] = h - vertical(u)
+        left_over = h - vertical(u)
+        for t in range(tiles):
+            at = pl.ds(x + nx * t, levels, stride=tiles * nx)
+            p_out[at, :] = u[:, 128 * t : 128 * t + 128]
+            r_out[at, :] = left_over[:, 128 * t : 128 * t + 128]
 
     for name in names:
         for copy, goes, _ in copies(name):
@@ -460,31 +487,32 @@
 
 def local(n_w, n_n, rhs, areas, stiffness):
     levels, nx, ny = rhs.shape
-    cx = nx // 2
+    cx, tiles = nx // 2, ny // 128
     steps = max(1, (n_w - 1).bit_length())
     vmem = lambda *shape: pltpu.VMEM(shape, f32)
     whole = pl.BlockSpec(memory_space=pltpu.VMEM)
-    return pl.pallas_call(
+    outs = pl.pallas_call(
         functools.partial(kernel, n_w, n_n, nx, ny, levels),
-        out_shape=[jax.ShapeDtypeStruct(rhs.shape, f32)] * 2,
+        out_shape=[jax.ShapeDtypeStruct((levels * nx * tiles, 128), f32)] * 2,
         in_specs=[whole, whole, pl.BlockSpec(memory_space=pltpu.SMEM)],
         out_specs=[whole, whole],
         scratch_shapes=[vmem(nx + 6, levels, ny)] * 6
         + [
             vmem(3 * nx, ny), vmem(cx + 8, levels, 128), vmem(cx + 8, levels, 128),
-            vmem(5, levels, 128), vmem(6, levels, 128), vmem(2, 2, levels, 128),
+            vmem(3, levels, 128), vmem(6, levels, 128), vmem(2, 2, 8, 128), vmem(2, 2, 8, 128),
             vmem(16, 128), vmem(2, 16, 128),
             vmem(steps, levels, 128), vmem(steps, levels, 128),
             vmem(steps, levels, 128), vmem(steps, levels, 128),
             vmem(levels, 128), vmem(levels, 128), vmem(levels, 128),
-            pltpu.SemaphoreType.DMA((9, 2)), pltpu.SemaphoreType.DMA((9, 2)),
+            pltpu.SemaphoreType.DMA((10, 2)), pltpu.SemaphoreType.DMA((10, 2)),
             pltpu.SemaphoreType.DMA((steps, 2)), pltpu.SemaphoreType.DMA((steps, 2)),
         ],
         compiler_params=pltpu.CompilerParams(
             collective_id=0, has_side_effects=True, vmem_limit_bytes=40 * 1024 * 1024
         ),
         cost_estimate=pl.CostEstimate(flops=80_000_000, bytes_accessed=1_600_000, transcendentals=0),
-    )(rhs, areas, stiffness)
+    )(rhs.reshape(levels, nx, tiles, 128).transpose(0, 2, 1, 3).reshape(-1, 128), areas, stiffness)
+    return tuple(v.reshape(levels, tiles, nx, 128).transpose(0, 2, 1, 3).reshape(rhs.shape) for v in outs)
 
 
 def solution(mesh):

time: 42 us -> 39.8 us (0.948)
  Pallas kernels: 37.2 us -> 34.9 us
    pallas_call x1, Pallas kernels: 37.2 us -> 34.9 us  [local(): pl.pallas_call(functools.partial(kernel, n_w, n_n, nx, ny, levels), out_s...]
where the time goes in v4:
time: 39.8 us; the launch traced here: 39.6 us
  Pallas kernels  34.9 us (88%)
  local copies, waits for them, and re-layouts  3.97 us (10%)
  between operations  0.65 us (2%)
    pallas_call x1, Pallas kernels, local(): pl.pallas_call(functools.partial(kernel, n_w, n_n, nx, ny, levels), out_s...  34.9 us
    unnamed x8, local copies, waits for them, and re-layouts  3.97 us

profile of v4, /device:TPU:1, one launch (start us, length us, event | category | flops | bytes accessed | tf_op | source)
XLA Modules:
  0.0 39.6 jit_solution(16619144216829538681)
XLA Ops:
  0.6 0.0 copy-start.2
  0.6 0.6 %copy-done.2 = f32[64]{0:T(128)S(1)} copy-done((f32[64]{0:T(128)S(1)}, f32[64]{0:T(128)}, u32[]{:S(2)}) %copy-start.2) | copy-done | bytes 280
  1.3 0.0 copy-start
  1.3 1.0 %copy-done = f32[64,8,256]{2,1,0:T(8,128)S(1)} copy-done((f32[64,8,256]{2,1,0:T(8,128)S(1)}, f32[64,8,256]{2,1,0:T(8,128)}, u32[]{:S(2)}) %copy-start) | copy-done | bytes 524312
  2.3 0.0 copy-start.1
  2.3 0.7 %copy-done.1 = f32[8,256]{1,0:T(8,128)S(1)} copy-done((f32[8,256]{1,0:T(8,128)S(1)}, f32[8,256]{1,0:T(8,128)}, u32[]{:S(2)}) %copy-start.1) | copy-done | bytes 8216
  3.0 34.9 %shard_map.50 = (f32[1024,128]{1,0:T(8,128)S(1)}, f32[1024,128]{1,0:T(8,128)S(1)}) custom-call(f32[1024,128]{1,0:T(8,128)S(1)} %bitcast.15, f32[8,256]{1,0:T(8,128)S(1)} %copy-done.1, f32[64]{0:T(128)S(1)} %copy-done.2), custom_call_target="tpu_custom_call" | custom-call | flops 80000000 | bytes 1600000 | tf_op jit(solution)/shard_map/pallas_call | solution.py:494
  38.0 0.8 %copy.7 = f32[64,8,256]{2,1,0:T(8,128)} copy(f32[64,8,256]{2,1,0:T(8,128)S(1)} %bitcast.17) | data formatting | bytes 1048576
  38.8 0.8 %copy.8 = f32[64,8,256]{2,1,0:T(8,128)} copy(f32[64,8,256]{2,1,0:T(8,128)S(1)} %bitcast.16) | data formatting | bytes 1048576
Async XLA Ops:
  0.6 0.7 %copy-start.2 = (f32[64]{0:T(128)S(1)}, f32[64]{0:T(128)}, u32[]{:S(2)}) copy-start(f32[64]{0:T(128)} %stiff_ref.1) | copy-start | bytes 772
  1.3 1.0 %copy-start = (f32[64,8,256]{2,1,0:T(8,128)S(1)}, f32[64,8,256]{2,1,0:T(8,128)}, u32[]{:S(2)}) copy-start(f32[64,8,256]{2,1,0:T(8,128)} %param.3) | copy-start | bytes 1572868
  2.3 0.7 %copy-start.1 = (f32[8,256]{1,0:T(8,128)S(1)}, f32[8,256]{1,0:T(8,128)}, u32[]{:S(2)}) copy-start(f32[8,256]{1,0:T(8,128)} %areas_ref.1) | copy-start | bytes 24580

commit v5 on v4

--- a/solution.py
+++ b/solution.py
@@ -19,7 +19,8 @@
 
 def kernel(
     n_w, n_n, nx, ny, levels,
-    rhs_ref, areas_ref, stiff_ref, p_out, r_out,
+    rhs_in, areas_in, stiff_in, p_out, r_out,
+    rhs_ref, stiff_ref, in_sem,
     rhs_x, u1, u2, u3, u4, p, wide_a, coarse, line, pack, strip, corner_of, corner, pack_a, strip_a,
     scan_f, scan_z, scan_rf, scan_rz, theta, phi, stiff_b,
     send_sem, recv_sem, scan_send, scan_recv,
@@ -39,6 +40,14 @@
     own = 3
     tiles = ny // 128
 
+    inputs = [
+        pltpu.make_async_copy(rhs_in, rhs_ref, in_sem.at[0]),
+        pltpu.make_async_copy(stiff_in, stiff_ref, in_sem.at[1]),
+        pltpu.make_async_copy(areas_in, wide_a.at[pl.ds(nx, nx)], in_sem.at[2]),
+    ]
+    for copy in inputs:
+        copy.start()
+
     small = jnp.zeros((levels, 128), f32)
     nothing = jnp.zeros((levels, ny), f32)
     edge_x = (
@@ -164,7 +173,7 @@
     def unsqueeze(tile, e):
         return jnp.concatenate([pltpu.roll(tile, (8 * e - 16 * b) % 128, 1) for b in range(levels // 8)], axis=0)
 
-    wide_a[nx : 2 * nx, :] = areas_ref[...]
+    inputs[0].wait()
     for x in (0, 1, nx - 2, nx - 1) + tuple(range(2, nx - 2)):
         rhs_x[own + x] = jnp.concatenate(
             [rhs_ref[pl.ds(x + nx * t, levels, stride=tiles * nx), :] for t in range(tiles)], axis=1
@@ -173,12 +182,14 @@
     for s in strides[1:]:
         peers = peers + (w >= s).astype(jnp.int32) + (w < n_w - s).astype(jnp.int32)
     pl.semaphore_wait(barrier, peers)
+    inputs[2].wait()
     start("areas")
     start("rhs")
     pack_rhs = packed([(e, rhs_x[e]) for e in range(own, own + nx)])
     pack[0] = pack_rhs
     start("strip")
 
+    inputs[1].wait()
     zero, one = jnp.float32(0.0), jnp.float32(1.0)
     t_before, t_now, p_before, p_now = zero, one, zero, one
     for i in range(levels):
@@ -485,6 +496,21 @@
             left.wait_send()
 
 
+def write(p_in, r_in, p_out, r_out, sem):
+    rows = p_in.shape[0] // 4
+    parts = [
+        pltpu.make_async_copy(
+            pair[0].at[pl.ds(rows * i, rows)], pair[1].at[pl.ds(rows * i, rows)], sem.at[4 * j + i]
+        )
+        for j, pair in enumerate(((p_in, p_out), (r_in, r_out)))
+        for i in range(4)
+    ]
+    for part in parts:
+        part.start()
+    for part in parts:
+        part.wait()
+
+
 def local(n_w, n_n, rhs, areas, stiffness):
     levels, nx, ny = rhs.shape
     cx, tiles = nx // 2, ny // 128
@@ -494,9 +520,12 @@
     outs = pl.pallas_call(
         functools.partial(kernel, n_w, n_n, nx, ny, levels),
         out_shape=[jax.ShapeDtypeStruct((levels * nx * tiles, 128), f32)] * 2,
-        in_specs=[whole, whole, pl.BlockSpec(memory_space=pltpu.SMEM)],
+        in_specs=[pl.BlockSpec(memory_space=pltpu.HBM)] * 3,
         out_specs=[whole, whole],
-        scratch_shapes=[vmem(nx + 6, levels, ny)] * 6
+        scratch_shapes=[
+            vmem(levels * nx * tiles, 128), pltpu.SMEM((levels,), f32), pltpu.SemaphoreType.DMA((3,)),
+        ]
+        + [vmem(nx + 6, levels, ny)] * 6
         + [
             vmem(3 * nx, ny), vmem(cx + 8, levels, 128), vmem(cx + 8, levels, 128),
             vmem(3, levels, 128), vmem(6, levels, 128), vmem(2, 2, 8, 128), vmem(2, 2, 8, 128),
@@ -508,10 +537,18 @@
             pltpu.SemaphoreType.DMA((steps, 2)), pltpu.SemaphoreType.DMA((steps, 2)),
         ],
         compiler_params=pltpu.CompilerParams(
-            collective_id=0, has_side_effects=True, vmem_limit_bytes=40 * 1024 * 1024
+            collective_id=0, has_side_effects=True, vmem_limit_bytes=56 * 1024 * 1024
         ),
         cost_estimate=pl.CostEstimate(flops=80_000_000, bytes_accessed=1_600_000, transcendentals=0),
     )(rhs.reshape(levels, nx, tiles, 128).transpose(0, 2, 1, 3).reshape(-1, 128), areas, stiffness)
+    outs = pl.pallas_call(
+        write,
+        out_shape=[jax.ShapeDtypeStruct((levels * nx * tiles, 128), f32)] * 2,
+        in_specs=[pl.BlockSpec(memory_space=pl.ANY)] * 2,
+        out_specs=[pl.BlockSpec(memory_space=pl.ANY)] * 2,
+        scratch_shapes=[pltpu.SemaphoreType.DMA((8,))],
+        compiler_params=pltpu.CompilerParams(vmem_limit_bytes=60 * 1024 * 1024),
+    )(*outs)
     return tuple(v.reshape(levels, tiles, nx, 128).transpose(0, 2, 1, 3).reshape(rhs.shape) for v in outs)
 
 

time: 39.8 us -> 69.2 us (1.74)
  Pallas kernels: 34.9 us -> 68.4 us
  local copies, waits for them, and re-layouts: 3.97 us -> 0 us
    pallas_call x0 -> x1, Pallas kernels: none -> 32.9 us  [local(): pl.pallas_call(write, out_shape=[jax.ShapeDtypeStruct((levels * nx * tile...]
    unnamed x8 -> x0, local copies, waits for them, and re-layouts: 3.97 us -> none
where the time goes in v5:
time: 69.2 us; the launch traced here: 69 us
  Pallas kernels  68.4 us (99%)
    pallas_call x1, Pallas kernels, local(): pl.pallas_call(functools.partial(kernel, n_w, n_n, nx, ny, levels), out_s...  35.4 us
    pallas_call x1, Pallas kernels, local(): pl.pallas_call(write, out_shape=[jax.ShapeDtypeStruct((levels * nx * tile...  32.9 us

profile of v5, /device:TPU:1, one launch (start us, length us, event | category | flops | bytes accessed | tf_op | source)
XLA Modules:
  0.0 69.0 jit_solution(14104193133066040764)
XLA Ops:
  0.6 35.4 %shard_map.50 = (f32[1024,128]{1,0:T(8,128)}, f32[1024,128]{1,0:T(8,128)}) custom-call(f32[1024,128]{1,0:T(8,128)} %bitcast.15, f32[8,256]{1,0:T(8,128)} %areas_in.1, f32[64]{0:T(128)} %stiff_in.1), custom_call_target="tpu_custom_call" | custom-call | flops 80000000 | bytes 1600000 | tf_op jit(solution)/shard_map/pallas_call | solution.py:520
  36.1 32.9 %shard_map.51 = (f32[1024,128]{1,0:T(8,128)}, f32[1024,128]{1,0:T(8,128)}) custom-call(f32[1024,128]{1,0:T(8,128)} %get-tuple-element.6.p_in, f32[1024,128]{1,0:T(8,128)} %get-tuple-element.7.r_in), custom_call_target="tpu_custom_call" | custom-call | tf_op jit(solution)/shard_map/pallas_call | solution.py:544

commit v6 on v5

--- a/solution.py
+++ b/solution.py
@@ -496,21 +496,6 @@
             left.wait_send()
 
 
-def write(p_in, r_in, p_out, r_out, sem):
-    rows = p_in.shape[0] // 4
-    parts = [
-        pltpu.make_async_copy(
-            pair[0].at[pl.ds(rows * i, rows)], pair[1].at[pl.ds(rows * i, rows)], sem.at[4 * j + i]
-        )
-        for j, pair in enumerate(((p_in, p_out), (r_in, r_out)))
-        for i in range(4)
-    ]
-    for part in parts:
-        part.start()
-    for part in parts:
-        part.wait()
-
-
 def local(n_w, n_n, rhs, areas, stiffness):
     levels, nx, ny = rhs.shape
     cx, tiles = nx // 2, ny // 128
@@ -541,14 +526,6 @@
         ),
         cost_estimate=pl.CostEstimate(flops=80_000_000, bytes_accessed=1_600_000, transcendentals=0),
     )(rhs.reshape(levels, nx, tiles, 128).transpose(0, 2, 1, 3).reshape(-1, 128), areas, stiffness)
-    outs = pl.pallas_call(
-        write,
-        out_shape=[jax.ShapeDtypeStruct((levels * nx * tiles, 128), f32)] * 2,
-        in_specs=[pl.BlockSpec(memory_space=pl.ANY)] * 2,
-        out_specs=[pl.BlockSpec(memory_space=pl.ANY)] * 2,
-        scratch_shapes=[pltpu.SemaphoreType.DMA((8,))],
-        compiler_params=pltpu.CompilerParams(vmem_limit_bytes=60 * 1024 * 1024),
-    )(*outs)
     return tuple(v.reshape(levels, tiles, nx, 128).transpose(0, 2, 1, 3).reshape(rhs.shape) for v in outs)
 
 

time: 69.2 us -> 39 us (0.56)
  Pallas kernels: 68.4 us -> 35.4 us
  local copies, waits for them, and re-layouts: 0 us -> 2.72 us
    pallas_call x1 -> x0, Pallas kernels: 32.9 us -> none  [local(): pl.pallas_call(write, out_shape=[jax.ShapeDtypeStruct((levels * nx * tile...]
    unnamed x0 -> x4, local copies, waits for them, and re-layouts: none -> 2.72 us
where the time goes in v6:
time: 39 us; the launch traced here: 38.8 us
  Pallas kernels  35.4 us (91%)
  local copies, waits for them, and re-layouts  2.72 us (7%)
  between operations  0.65 us (2%)
    pallas_call x1, Pallas kernels, local(): pl.pallas_call(functools.partial(kernel, n_w, n_n, nx, ny, levels), out_s...  35.4 us
    unnamed x4, local copies, waits for them, and re-layouts  2.72 us

profile of v6, /device:TPU:1, one launch (start us, length us, event | category | flops | bytes accessed | tf_op | source)
XLA Modules:
  0.0 38.8 jit_solution(5582307509153860064)
XLA Ops:
  0.6 35.4 %shard_map.50 = (f32[1024,128]{1,0:T(8,128)}, f32[1024,128]{1,0:T(8,128)}) custom-call(f32[1024,128]{1,0:T(8,128)} %bitcast.15, f32[8,256]{1,0:T(8,128)} %areas_in.1, f32[64]{0:T(128)} %stiff_in.1), custom_call_target="tpu_custom_call" | custom-call | flops 80000000 | bytes 1600000 | tf_op jit(solution)/shard_map/pallas_call | solution.py:505
  36.1 0.0 copy-start
  36.1 1.9 %copy.7 = f32[64,8,256]{2,1,0:T(8,128)} copy(f32[64,8,256]{2,1,0:T(8,128)} %bitcast.17) | data formatting | bytes 1048576
  38.0 0.0 copy-done
  38.0 0.8 %copy.8 = f32[64,8,256]{2,1,0:T(8,128)} copy(f32[64,8,256]{2,1,0:T(8,128)S(1)} %bitcast.16) | data formatting | bytes 1048576
Async XLA Ops:
  36.1 1.9 %copy-start = (f32[1024,128]{1,0:T(8,128)S(1)}, f32[1024,128]{1,0:T(8,128)}, u32[]{:S(2)}) copy-start(f32[1024,128]{1,0:T(8,128)} %get-tuple-element.5) | copy-start | bytes 1572868
